TPU v7x, 256 devices: a whole 4x4x8 slice. The times are simulated.
256 devices in a mesh: stream: 32 (over z, x_hi, core), span: 8 (over y, x_lo).
Axes of the slice: x: 4 (x_hi: 2, x_lo: 2; x = x_hi * 2 + x_lo), y: 4, z: 8, core: 2. Of those that a mesh axis runs over, the one named last changes fastest.
Arguments:
- adjoint: bfloat16 [192, 128, 128, 128], P(None, 'stream', 'span'), may hold values from -6 to 6
- velocity: bfloat16 [192, 128, 128, 128], P(None, 'stream', 'span'), may hold values from -6 to 6
- density: float32 [128, 128, 128], P('stream', 'span'), may hold values from 0 to 1
- metric: float32 [128, 128, 128], P('stream', 'span'), may hold values from 0.5 to 2
- orientation: int32 [6, 128, 128, 128], P(None, 'stream', 'span'), may hold values from 0 to 1
- design_ids: int32 [128, 128, 128], P('stream', 'span'), may hold values from 0 to 4
- volume_block: bfloat16 [192, 192], replicated, may hold values from -0.4375 to 0.4375
- face_trace: bfloat16 [6, 48, 192], replicated, may hold values from -0.4375 to 0.4375
- face_lift: bfloat16 [6, 192, 48], replicated, may hold values from -0.875 to 0.875
Outputs:
- residual: bfloat16 [192, 128, 128, 128], P(None, 'stream', 'span')
- filtered: float32 [128, 128, 128], P('stream', 'span')
- volumes: float32 [4], replicated
All inputs are finite; a program needn't handle non-finite values.
Results may differ from a plain program's by a relative error of at most 0.0043.
Values may be sent and summed in bfloat16 or wider, within the bound.
A program may use at most 128 MiB of HBM per device.

v0:
```python
import jax
import jax.numpy as jnp
from jax import lax
from jax.sharding import PartitionSpec as P

GROUPS = 4


sens_scale = 0.03125
filter_beta = 0.5


def extended(cells, sides, width, closed):
    for axis, dim in sides:
        count = lax.axis_size(axis)
        ends = count if closed else count - 1
        head = lax.slice_in_dim(cells, 0, width, axis=dim)
        tail = lax.slice_in_dim(cells, cells.shape[dim] - width, cells.shape[dim], axis=dim)
        cells = jnp.concatenate(
            [
                lax.ppermute(tail, axis, [(i, (i + 1) % count) for i in range(ends)]),
                cells,
                lax.ppermute(head, axis, [((i + 1) % count, i) for i in range(ends)]),
            ],
            axis=dim,
        )
    return cells


def along_depth(field):
    zeros = jnp.zeros_like(field[..., :1])
    lower = jnp.concatenate([zeros, field[..., :-1]], axis=-1)
    upper = jnp.concatenate([field[..., 1:], zeros], axis=-1)
    return (lower, upper)


def apply_trace(block, values):
    return jnp.einsum("ti,ixyz->txyz", block, values, preferred_element_type=jnp.float32).astype(
        jnp.bfloat16
    )


def edge_pair(first, last, axis):
    return jnp.concatenate([first, last], axis=axis)


def shards(
    adjoint, velocity, density, metric, orientation, design_ids, volume_block, face_trace, face_lift
):
    alpha = 2.0 * (1.0 - density) / (1.0 + density)
    slope = -4.0 / ((1.0 + density) * (1.0 + density))
    inner = jnp.einsum("ixyz,ixyz->xyz", velocity, adjoint, preferred_element_type=jnp.float32)
    live = (design_ids > 0).astype(jnp.float32)
    sensitivity = (live * slope * metric * inner * sens_scale).astype(jnp.bfloat16)[None]
    traces = jnp.einsum(
        "kti,ixyz->ktxyz", face_trace, adjoint, preferred_element_type=jnp.float32
    ).astype(jnp.bfloat16)
    stream_send = edge_pair(adjoint[:, :1], adjoint[:, -1:], 1)
    span_send = edge_pair(adjoint[:, :, :1], adjoint[:, :, -1:], 2)
    stream_sens_send = edge_pair(sensitivity[:, :1], sensitivity[:, -1:], 1)
    span_sens_send = edge_pair(sensitivity[:, :, :1], sensitivity[:, :, -1:], 2)
    stream_got = extended(stream_send, (("stream", 1),), 1, True)
    span_got = extended(span_send, (("span", 2),), 1, False)
    total = jnp.einsum("ij,ixyz->jxyz", volume_block, adjoint, preferred_element_type=jnp.float32)
    total = metric[None] * (total + alpha[None] * adjoint.astype(jnp.float32))
    low_x = stream_got[:, :1]
    high_x = stream_got[:, 3:]
    low_y = span_got[:, :, :1]
    high_y = span_got[:, :, 3:]
    low_x = apply_trace(face_trace[0], low_x)
    high_x = apply_trace(face_trace[1], high_x)
    low_y = apply_trace(face_trace[2], low_y)
    high_y = apply_trace(face_trace[3], high_y)
    lower_z, _ = along_depth(traces[4])
    _, upper_z = along_depth(traces[5])
    neighbours = [
        jnp.concatenate([low_x, traces[0][:, :-1]], axis=1),
        jnp.concatenate([traces[1][:, 1:], high_x], axis=1),
        jnp.concatenate([low_y, traces[2][:, :, :-1]], axis=2),
        jnp.concatenate([traces[3][:, :, 1:], high_y], axis=2),
        lower_z,
        upper_z,
    ]
    signs = 1.0 - 2.0 * orientation.astype(jnp.float32)
    for face in range(6):
        lifted = jnp.einsum(
            "jt,txyz->jxyz", face_lift[face], neighbours[face], preferred_element_type=jnp.float32
        )
        total = total + signs[face][None] * lifted
    residual = total.astype(jnp.bfloat16)
    stream_sens = extended(stream_sens_send, (("stream", 1),), 1, True)
    span_sens = extended(span_sens_send, (("span", 2),), 1, False)
    own = sensitivity.astype(jnp.float32)
    lower_s, upper_s = along_depth(own)
    beside_all = jnp.concatenate([stream_sens[:, :1].astype(jnp.float32), own[:, :-1]], axis=1)
    beside_all = beside_all + jnp.concatenate(
        [own[:, 1:], stream_sens[:, 3:].astype(jnp.float32)], axis=1
    )
    beside_all = beside_all + jnp.concatenate(
        [span_sens[:, :, :1].astype(jnp.float32), own[:, :, :-1]], axis=2
    )
    beside_all = beside_all + jnp.concatenate(
        [own[:, :, 1:], span_sens[:, :, 3:].astype(jnp.float32)], axis=2
    )
    beside_all = beside_all + lower_s + upper_s
    filtered = ((own + filter_beta * beside_all) / (1.0 + 6.0 * filter_beta))[0]
    weighted = density * metric
    labels = jnp.arange(1, GROUPS + 1, dtype=jnp.int32)
    partial_value = jnp.sum(
        jnp.where(
            design_ids[None] == labels[:, None, None, None], weighted[None], jnp.float32(0.0)
        ),
        axis=(1, 2, 3),
    )
    volumes = lax.psum(partial_value, ("stream", "span")) / jnp.float32(density.size)
    return (residual, filtered, volumes)


def solution(mesh):
    return jax.shard_map(
        shards,
        mesh=mesh,
        in_specs=(
            P(None, "stream", "span", None),
            P(None, "stream", "span", None),
            P("stream", "span", None),
            P("stream", "span", None),
            P(None, "stream", "span", None),
            P("stream", "span", None),
            P(),
            P(),
            P(),
        ),
        out_specs=(P(None, "stream", "span", None), P("stream", "span", None), P()),
        check_vma=False,
    )
```

profile of v0, /device:TPU:1, one launch (start us, length us, event | category | flops | bytes accessed | tf_op | source)
XLA Modules:
  0.0 179.8 jit_solution(7849650485327796674)
XLA Ops:
  0.6 0.0 copy-start
  0.6 0.0 copy-start.1
  0.7 0.0 copy-start.12
  0.7 0.0 copy-start.7
  0.7 0.0 copy-start.15
  0.7 0.0 copy-start.5
  0.7 4.3 %fusion = f32[4,16,128]{2,1,0:T(8,128)S(1)} fusion(bf16[192,4,16,128]{3,2,1,0:T(8,128)(2,1)} %param.9, bf16[192,4,16,128]{3,2,1,0:T(8,128)(2,1)} %param.10), kind=kLoop, calls=%fused_computation.1 | loop fusion | flops 6283264 | bytes 6324224 | tf_op jit(solution)/shard_map/ixyz,ixyz->xyz/dot_general | solution.py:52
  5.0 0.0 copy-done.12
  5.0 0.0 copy-done.7
  5.0 0.6 fusion.76
  5.7 0.6 fusion.79
  6.3 1.3 collective-permute-start.7
  7.5 5.2 %collective-permute-start.6 = (bf16[1,4,1,128]{3,2,1,0:T(2,128)(2,1)}, bf16[1,4,1,128]{3,2,1,0:T(2,128)(2,1)}, u32[]{:S(2)}, u32[]{:S(2)}) collective-permute-start(bf16[1,4,1,128]{3,2,1,0:T(2,128)(2,1)} %get-tuple-element.33), channel_id=1, source_target_pairs={{0,1},{1,2},{2,3},{3,4},{4,5},{5,6},{6,7},{8,9},{9,10},{10,11},{11... | collective-permute-start | bytes 3080 | tf_op jit(solution)/shard_map/ppermute | solution.py:21
  12.7 3.2 %collective-permute-start.5 = (bf16[1,1,16,128]{3,2,1,0:T(8,128)(2,1)S(1)}, bf16[1,1,16,128]{3,2,1,0:T(8,128)(2,1)S(1)}, u32[]{:S(2)}, u32[]{:S(2)}) collective-permute-start(bf16[1,1,16,128]{3,2,1,0:T(8,128)(2,1)S(1)} %get-tuple-element.36), channel_id=1, source_target_pairs={{8,0},{16,8},{24,16},{32,24},{40,32},{48,40},{56,48},{64,56},{72,6... | collective-permute-start | bytes 12296 | tf_op jit(solution)/shard_map/ppermute | solution.py:23
  15.9 0.9 collective-permute-start.4
  16.8 1.3 fusion.75
  18.2 0.7 copy.47
  18.9 1.3 collective-permute-start.3
  20.2 0.6 fusion.78
  20.8 0.7 fusion.77
  21.5 1.5 fusion.74
  23.0 0.2 select_reduce_fusion
  23.2 0.6 fusion.80
  23.8 83.9 %psum.7 = f32[4]{0:T(128)} all-reduce(f32[4]{0:T(128)S(1)} %select_reduce_fusion), channel_id=1, replica_groups=mesh['stream'=32,'span'=8] {'stream','span'}, use_global_device_ids=true, to_apply=%region_1.2 | all-reduce | flops 4 | bytes 32 | tf_op jit(solution)/shard_map/psum | solution.py:115
  107.7 0.9 multiply_subtract_fusion
  108.6 0.6 slice_bitcast_fusion.11
  109.2 2.8 %fusion.4 = bf16[6,48,4,16,128]{4,1,3,2,0:T(8,128)(2,1)S(1)} fusion(bf16[6,48,192]{2,1,0:T(8,128)(2,1)S(1)} %copy-done.5, bf16[192,4,16,128]{3,2,1,0:T(8,128)(2,1)S(1)} %copy-done.1), kind=kOutput, calls=%fused_computation.11 | convolution fusion | flops 908328960 | bytes 7974912 | tf_op jit(solution)/shard_map/kti,ixyz->ktxyz/dot_general | solution.py:55
  112.0 0.0 copy-start.6
  112.0 1.3 slice_bitcast_fusion.5
  113.4 0.3 slice.187
  113.7 0.0 copy-start.16
  113.7 0.0 copy-start.4
  113.7 0.0 copy-start.3
  113.7 3.7 %fusion.29 = f32[4,16,128,192]{2,3,1,0:T(8,128)} fusion(bf16[48,4,16,127]{3,0,2,1:T(8,128)(2,1)S(1)} %slice.187, bf16[6,192,48]{1,2,0:T(8,128)(2,1)S(1)} %copy-done.6), kind=kOutput, calls=%fused_computation.44 | convolution fusion | flops 150994944 | bytes 7102464 | tf_op jit(solution)/shard_map/jt,txyz->jxyz/dot_general | solution.py:86
  117.4 3.7 %fusion.31 = f32[4,16,128,192]{2,3,1,0:T(8,128)} fusion(bf16[48,4,16,127]{3,0,2,1:T(8,128)(2,1)S(1)} %bitcast.148, bf16[6,192,48]{1,2,0:T(8,128)(2,1)S(1)} %copy-done.6), kind=kOutput, calls=%fused_computation.46 | convolution fusion | flops 150994944 | bytes 7102464 | tf_op jit(solution)/shard_map/jt,txyz->jxyz/dot_general | solution.py:86
  121.1 0.5 broadcast_multiply_fusion
  121.6 0.2 copy.55
  121.8 0.2 copy.54
  122.2 0.1 slice.181
  122.2 0.1 slice.178
  122.3 0.0 collective-permute-done.7
  122.3 1.5 collective-permute-start.2
  123.8 0.7 convert_element_type.76
  124.5 0.0 collective-permute-done.6
  124.5 0.9 collective-permute-start.1
  125.4 0.7 convert_element_type.75
  126.1 0.0 collective-permute-done.5
  126.1 2.3 %collective-permute-start = (bf16[192,1,16,128]{3,0,2,1:T(8,128)(2,1)S(1)}, bf16[192,1,16,128]{3,0,2,1:T(8,128)(2,1)S(1)}, u32[]{:S(2)}, u32[]{:S(2)}) collective-permute-start(bf16[192,1,16,128]{3,0,2,1:T(8,128)(2,1)S(1)} %copy.55), channel_id=1, source_target_pairs={{0,8},{8,16},{16,24},{24,32},{32,40},{40,48},{48,56},{56,64},{64,7... | collective-permute-start | bytes 2359304 | tf_op jit(solution)/shard_map/ppermute | solution.py:21
  128.4 0.0 collective-permute-done.4
  128.5 0.7 fusion.44
  129.2 0.0 collective-permute-done.3
  129.2 1.1 fusion.10
  130.3 0.0 collective-permute-done.2
  130.3 0.1 fusion.9
  130.4 3.7 %fusion.19 = f32[4,16,128,192]{2,3,1,0:T(8,128)} fusion(bf16[48,4,15,128]{3,0,2,1:T(8,128)(2,1)S(1)} %slice.178, bf16[48,4,1,128]{3,0,2,1:T(8,128)(2,1)S(1)} %fusion.9, bf16[6,192,48]{1,2,0:T(8,128)(2,1)S(1)} %copy-done.6), kind=kOutput, calls=%fused_computation.34 | convolution fusion | flops 151388160 | bytes 7102464 | tf_op jit(solution)/shard_map/jt,txyz->jxyz/dot_general | solution.py:86
  134.1 3.6 %fusion.23 = f32[4,16,128,192]{2,3,1,0:T(8,128)} fusion(bf16[48,4,1,128]{3,0,2,1:T(8,128)(2,1)S(1)} %fusion.10, bf16[48,4,15,128]{3,0,2,1:T(8,128)(2,1)S(1)} %slice.181, bf16[6,192,48]{1,2,0:T(8,128)(2,1)S(1)} %copy-done.6), kind=kOutput, calls=%fused_computation.38 | convolution fusion | flops 151388160 | bytes 7102464 | tf_op jit(solution)/shard_map/jt,txyz->jxyz/dot_general | solution.py:86
  137.7 10.5 %collective-permute-done.1 = bf16[192,1,16,128]{3,0,2,1:T(8,128)(2,1)S(1)} collective-permute-done((bf16[192,1,16,128]{3,0,2,1:T(8,128)(2,1)S(1)}, bf16[192,1,16,128]{3,0,2,1:T(8,128)(2,1)S(1)}, u32[]{:S(2)}, u32[]{:S(2)}) %collective-permute-start.1) | collective-permute-done | bytes 786464 | tf_op jit(solution)/shard_map/ppermute | solution.py:23
  148.2 0.3 fusion.8
  148.5 3.7 %fusion.15 = f32[4,16,128,192]{2,3,1,0:T(8,128)} fusion(bf16[48,1,16,128]{3,0,2,1:T(8,128)(2,1)S(1)} %fusion.8, bf16[48,3,16,128]{3,0,2,1:T(8,128)(2,1)S(1)} %slice.174, bf16[6,192,48]{1,2,0:T(8,128)(2,1)S(1)} %copy-done.6), kind=kOutput, calls=%fused_computation.30 | convolution fusion | flops 151388160 | bytes 7102464 | tf_op jit(solution)/shard_map/jt,txyz->jxyz/dot_general | solution.py:86
  152.2 0.0 collective-permute-done
  152.2 0.3 fusion.7
  152.4 3.7 %fusion.11 = f32[4,16,128,192]{2,3,1,0:T(8,128)} fusion(bf16[48,3,16,128]{3,0,2,1:T(8,128)(2,1)S(1)} %slice.171, bf16[48,1,16,128]{3,0,2,1:T(8,128)(2,1)S(1)} %fusion.7, bf16[6,192,48]{1,2,0:T(8,128)(2,1)S(1)} %copy-done.6), kind=kOutput, calls=%fused_computation.26 | convolution fusion | flops 151388160 | bytes 7102464 | tf_op jit(solution)/shard_map/jt,txyz->jxyz/dot_general | solution.py:86
  156.2 18.0 %fusion.1 = bf16[192,4,16,128]{3,0,2,1:T(8,128)(2,1)} fusion(f32[4,16,128,192]{2,3,1,0:T(8,128)} %fusion.29, f32[4,16,128,192]{2,3,1,0:T(8,128)} %fusion.31, f32[4,16,128,192]{2,3,1,0:T(8,128)} %fusion.23, f32[4,16,128,192]{2,3,1,0:T(8,128)} %fusion.19, f32[4,16,128,192]{2,3,1,0:T(8,128)} %fusion.15, f32[4,16,128,192]{2,3,1,0:T(8,128)} %fusion.11, ...), kind=kOutput, calls=%fused_computation.3 | convolution fusion | flops 630718464 | bytes 44376064 | tf_op jit(solution)/shard_map/ij,ixyz->jxyz/dot_general | solution.py:64
  174.2 5.6 %copy.29 = bf16[192,4,16,128]{3,2,1,0:T(8,128)(2,1)} copy(bf16[192,4,16,128]{3,0,2,1:T(8,128)(2,1)} %fusion.1) | data formatting | bytes 6291456
  (29 shorter events, 0.2 us)
Async XLA Ops:
  0.6 155.6 %copy-start = (bf16[192,192]{1,0:T(8,128)(2,1)S(1)}, bf16[192,192]{1,0:T(8,128)(2,1)}, u32[]{:S(2)}) copy-start(bf16[192,192]{1,0:T(8,128)(2,1)} %param.15) | copy-start | bytes 221188
  0.6 16.2 %copy-start.1 = (bf16[192,4,16,128]{3,2,1,0:T(8,128)(2,1)S(1)}, bf16[192,4,16,128]{3,2,1,0:T(8,128)(2,1)}, u32[]{:S(2)}) copy-start(bf16[192,4,16,128]{3,2,1,0:T(8,128)(2,1)} %param.9) | copy-start | bytes 9437188
  0.7 4.3 %copy-start.12 = (s32[4,16,128]{2,1,0:T(8,128)S(1)}, s32[4,16,128]{2,1,0:T(8,128)}, u32[]{:S(2)}) copy-start(s32[4,16,128]{2,1,0:T(8,128)} %param.14) | copy-start | bytes 98308
  0.7 4.3 %copy-start.7 = (f32[4,16,128]{2,1,0:T(8,128)S(1)}, f32[4,16,128]{2,1,0:T(8,128)}, u32[]{:S(2)}) copy-start(f32[4,16,128]{2,1,0:T(8,128)} %param.12) | copy-start | bytes 98308
  0.7 4.3 %copy-start.15 = (f32[4,16,128]{2,1,0:T(8,128)S(1)}, f32[4,16,128]{2,1,0:T(8,128)}, u32[]{:S(2)}) copy-start(f32[4,16,128]{2,1,0:T(8,128)} %param.11) | copy-start | bytes 98308
  0.7 108.6 %copy-start.5 = (bf16[6,48,192]{2,1,0:T(8,128)(2,1)S(1)}, bf16[6,48,192]{2,1,0:T(8,128)(2,1)}, u32[]{:S(2)}) copy-start(bf16[6,48,192]{2,1,0:T(8,128)(2,1)} %param.16) | copy-start | bytes 331780
  6.3 116.0 %collective-permute-start.7 = (bf16[1,4,1,128]{3,2,1,0:T(2,128)(2,1)}, bf16[1,4,1,128]{3,2,1,0:T(2,128)(2,1)}, u32[]{:S(2)}, u32[]{:S(2)}) collective-permute-start(bf16[1,4,1,128]{3,2,1,0:T(2,128)(2,1)} %get-tuple-element.32), channel_id=1, source_target_pairs={{1,0},{2,1},{3,2},{4,3},{5,4},{6,5},{7,6},{9,8},{10,9},{11,10},{12... | collective-permute-start | bytes 3080 | tf_op jit(solution)/shard_map/ppermute | solution.py:23
  7.5 116.9 %collective-permute-start.6 = (bf16[1,4,1,128]{3,2,1,0:T(2,128)(2,1)}, bf16[1,4,1,128]{3,2,1,0:T(2,128)(2,1)}, u32[]{:S(2)}, u32[]{:S(2)}) collective-permute-start(bf16[1,4,1,128]{3,2,1,0:T(2,128)(2,1)} %get-tuple-element.33), channel_id=1, source_target_pairs={{0,1},{1,2},{2,3},{3,4},{4,5},{5,6},{6,7},{8,9},{9,10},{10,11},{11... | collective-permute-start | bytes 3080 | tf_op jit(solution)/shard_map/ppermute | solution.py:21
  12.7 113.4 %collective-permute-start.5 = (bf16[1,1,16,128]{3,2,1,0:T(8,128)(2,1)S(1)}, bf16[1,1,16,128]{3,2,1,0:T(8,128)(2,1)S(1)}, u32[]{:S(2)}, u32[]{:S(2)}) collective-permute-start(bf16[1,1,16,128]{3,2,1,0:T(8,128)(2,1)S(1)} %get-tuple-element.36), channel_id=1, source_target_pairs={{8,0},{16,8},{24,16},{32,24},{40,32},{48,40},{56,48},{64,56},{72,6... | collective-permute-start | bytes 12296 | tf_op jit(solution)/shard_map/ppermute | solution.py:23
  15.9 112.5 %collective-permute-start.4 = (bf16[1,1,16,128]{3,2,1,0:T(8,128)(2,1)S(1)}, bf16[1,1,16,128]{3,2,1,0:T(8,128)(2,1)S(1)}, u32[]{:S(2)}, u32[]{:S(2)}) collective-permute-start(bf16[1,1,16,128]{3,2,1,0:T(8,128)(2,1)S(1)} %get-tuple-element.37), channel_id=1, source_target_pairs={{0,8},{8,16},{16,24},{24,32},{32,40},{40,48},{48,56},{56,64},{64,7... | collective-permute-start | bytes 12296 | tf_op jit(solution)/shard_map/ppermute | solution.py:21
  18.9 110.3 %collective-permute-start.3 = (bf16[192,4,1,128]{3,0,1,2:T(8,128)(2,1)}, bf16[192,4,1,128]{3,0,1,2:T(8,128)(2,1)}, u32[]{:S(2)}, u32[]{:S(2)}) collective-permute-start(bf16[192,4,1,128]{3,0,1,2:T(8,128)(2,1)} %copy.47), channel_id=1, source_target_pairs={{1,0},{2,1},{3,2},{4,3},{5,4},{6,5},{7,6},{9,8},{10,9},{11,10},{12... | collective-permute-start | bytes 589832 | tf_op jit(solution)/shard_map/ppermute | solution.py:23
  112.0 1.6 copy-start.6
  113.7 7.4 %copy-start.16 = (f32[4]{0:T(128)S(1)}, f32[4]{0:T(128)}, u32[]{:S(2)}) copy-start(f32[4]{0:T(128)} %psum.7) | copy-start | bytes 52
  113.7 7.9 %copy-start.4 = (bf16[192,4,1,128]{3,2,1,0:T(2,128)(2,1)S(1)}, bf16[192,4,1,128]{3,2,1,0:T(2,128)(2,1)}, u32[]{:S(2)}) copy-start(bf16[192,4,1,128]{3,2,1,0:T(2,128)(2,1)} %get-tuple-element.17) | copy-start | bytes 589828
  113.7 7.9 %copy-start.3 = (bf16[192,1,16,128]{3,2,1,0:T(8,128)(2,1)S(1)}, bf16[192,1,16,128]{3,2,1,0:T(8,128)(2,1)}, u32[]{:S(2)}) copy-start(bf16[192,1,16,128]{3,2,1,0:T(8,128)(2,1)} %get-tuple-element.15) | copy-start | bytes 2359300
  117.4 4.5 %copy-start.2 = (bf16[192,1,16,128]{3,2,1,0:T(8,128)(2,1)S(1)}, bf16[192,1,16,128]{3,2,1,0:T(8,128)(2,1)}, u32[]{:S(2)}) copy-start(bf16[192,1,16,128]{3,2,1,0:T(8,128)(2,1)} %get-tuple-element.16) | copy-start | bytes 2359300
  121.0 7.4 %copy-start.8 = (f32[1,4,15,128]{3,2,1,0:T(8,128)S(1)}, f32[1,4,15,128]{3,2,1,0:T(8,128)}, u32[]{:S(2)}) copy-start(f32[1,4,15,128]{3,2,1,0:T(8,128)} %get-tuple-element.30) | copy-start | bytes 92164
  121.0 7.4 %copy-start.9 = (f32[1,4,15,128]{3,2,1,0:T(8,128)S(1)}, f32[1,4,15,128]{3,2,1,0:T(8,128)}, u32[]{:S(2)}) copy-start(f32[1,4,15,128]{3,2,1,0:T(8,128)} %get-tuple-element.31) | copy-start | bytes 92164
  121.0 7.4 %copy-start.10 = (f32[1,4,16,127]{3,2,1,0:T(8,128)S(1)}, f32[1,4,16,127]{3,2,1,0:T(8,128)}, u32[]{:S(2)}) copy-start(f32[1,4,16,127]{3,2,1,0:T(8,128)} %get-tuple-element.28) | copy-start | bytes 97540
  121.0 7.4 %copy-start.11 = (f32[1,4,16,127]{3,2,1,0:T(8,128)S(1)}, f32[1,4,16,127]{3,2,1,0:T(8,128)}, u32[]{:S(2)}) copy-start(f32[1,4,16,127]{3,2,1,0:T(8,128)} %get-tuple-element.29) | copy-start | bytes 97540
  121.0 7.4 %copy-start.13 = (f32[1,3,16,128]{3,2,1,0:T(8,128)S(1)}, f32[1,3,16,128]{3,2,1,0:T(8,128)}, u32[]{:S(2)}) copy-start(f32[1,3,16,128]{3,2,1,0:T(8,128)} %get-tuple-element.34) | copy-start | bytes 73732
  121.1 7.4 %copy-start.14 = (f32[1,3,16,128]{3,2,1,0:T(8,128)S(1)}, f32[1,3,16,128]{3,2,1,0:T(8,128)}, u32[]{:S(2)}) copy-start(f32[1,3,16,128]{3,2,1,0:T(8,128)} %get-tuple-element.35) | copy-start | bytes 73732
  122.3 8.0 %collective-permute-start.2 = (bf16[192,4,1,128]{3,0,1,2:T(8,128)(2,1)S(1)}, bf16[192,4,1,128]{3,0,1,2:T(8,128)(2,1)S(1)}, u32[]{:S(2)}, u32[]{:S(2)}) collective-permute-start(bf16[192,4,1,128]{3,0,1,2:T(8,128)(2,1)S(1)} %copy.46), channel_id=1, source_target_pairs={{0,1},{1,2},{2,3},{3,4},{4,5},{5,6},{6,7},{8,9},{9,10},{10,11},{11... | collective-permute-start | bytes 589832 | tf_op jit(solution)/shard_map/ppermute | solution.py:21
  124.5 23.7 %collective-permute-start.1 = (bf16[192,1,16,128]{3,0,2,1:T(8,128)(2,1)S(1)}, bf16[192,1,16,128]{3,0,2,1:T(8,128)(2,1)S(1)}, u32[]{:S(2)}, u32[]{:S(2)}) collective-permute-start(bf16[192,1,16,128]{3,0,2,1:T(8,128)(2,1)S(1)} %copy.54), channel_id=1, source_target_pairs={{8,0},{16,8},{24,16},{32,24},{40,32},{48,40},{56,48},{64,56},{72,6... | collective-permute-start | bytes 2359304 | tf_op jit(solution)/shard_map/ppermute | solution.py:23
  126.1 26.1 %collective-permute-start = (bf16[192,1,16,128]{3,0,2,1:T(8,128)(2,1)S(1)}, bf16[192,1,16,128]{3,0,2,1:T(8,128)(2,1)S(1)}, u32[]{:S(2)}, u32[]{:S(2)}) collective-permute-start(bf16[192,1,16,128]{3,0,2,1:T(8,128)(2,1)S(1)} %copy.55), channel_id=1, source_target_pairs={{0,8},{8,16},{16,24},{24,32},{32,40},{40,48},{48,56},{56,64},{64,7... | collective-permute-start | bytes 2359304 | tf_op jit(solution)/shard_map/ppermute | solution.py:21
where the time goes:
time: 180 us
  blocking collectives  83.9 us (47%)
  matrix products  44.5 us (25%)
  starting transfers between devices  16.6 us (9%)
  local copies, waits for them, and re-layouts  14.6 us (8%)
  waiting for transfers between devices  10.5 us (6%)
  other arithmetic  8.65 us (5%)
    psum x1, blocking collectives, shards(): lax.psum(partial_value, ('stream', 'span')) / jnp.float32(density.size)  83.9 us
    dot_general x6, matrix products, shards(): jnp.einsum('jt,txyz->jxyz', face_lift[face], neighbours[face], preferred_...  22.1 us
    dot_general x1, matrix products, shards(): jnp.einsum('ij,ixyz->jxyz', volume_block, adjoint, preferred_element_type...  18 us
    ppermute x4, waiting for transfers between devices, extended(): lax.ppermute(head, axis, [((i + 1) % count, i) for i in range(ends)])  10.5 us
    ppermute x4, starting transfers between devices, extended(): lax.ppermute(tail, axis, [(i, (i + 1) % count) for i in range(ends)])  9.89 us
    unnamed x39, local copies, waits for them, and re-layouts  6.82 us
    ppermute x4, starting transfers between devices, extended(): lax.ppermute(head, axis, [((i + 1) % count, i) for i in range(ends)])  6.71 us
    dot_general x1, other arithmetic, shards(): jnp.einsum('ixyz,ixyz->xyz', velocity, adjoint, preferred_element_type=jn...  4.29 us
  transfers between devices with their start and end apart: 8, of which 1 were waited for; matrix products, arithmetic and copies ran while one was open for 19% of the time, Pallas kernels for 0%

commit v1 on v0

v1 whole, which is shorter than its diff:
```python
import functools

import jax
import jax.numpy as jnp
from jax import lax
from jax.experimental import pallas as pl
from jax.experimental.pallas import tpu as pltpu
from jax.sharding import PartitionSpec as P

MESH = pl.DeviceIdType.MESH
F32 = jnp.float32
BF16 = jnp.bfloat16
GROUPS = 4
SENS_SCALE = 0.03125
FILTER_BETA = 0.5
ROWS = 48
CHUNK = 4


def shift_rows(field, first, up):
    row = lax.broadcasted_iota(jnp.int32, field.shape, 0)
    edge = field.shape[0] - 1 if up else 0
    moved = pltpu.roll(field, field.shape[0] - 1 if up else 1, 0)
    return jnp.where(row == edge, first, moved)


def shift_lanes(field, up):
    lane = lax.broadcasted_iota(jnp.int32, field.shape, field.ndim - 1)
    edge = 127 if up else 0
    moved = pltpu.roll(field, 127 if up else 1, field.ndim - 1)
    return jnp.where(lane == edge, jnp.zeros_like(field), moved)


def first_kernel(
    n_stream, n_span, remote,
    adj_hbm, vel_hbm, den_hbm, met_hbm, ids_hbm, vol_hbm, trace_hbm,
    base, tx0, tx1, ty2, ty3, tz4, tz5, sens, sx_lo, sx_hi, sy_lo, sy_hi, vol_out,
    adj, vel, den, met, ids, vol, weights, send_lo, send_hi, slots_a, slots_b, part_a, part_b,
    in_sem, vel_sem, small_sem, halo_send, halo_recv, a_send, a_recv, b_send, b_recv,
):
    cx = adj.shape[1]
    stream, span = lax.axis_index("stream"), lax.axis_index("span")

    if remote:
        barrier = pltpu.get_barrier_semaphore()

        def greet_span(d, _):
            pl.semaphore_signal(barrier, inc=1, device_id=(stream, lax.rem(span + d, n_span)), device_id_type=MESH)
            return 0

        def greet_stream(d, _):
            pl.semaphore_signal(barrier, inc=1, device_id=(lax.rem(stream + d, n_stream), span), device_id_type=MESH)
            return 0

    trace_copy = pltpu.make_async_copy(trace_hbm, weights.at[pl.ds(192, 288)], small_sem.at[0])
    vol_copy = pltpu.make_async_copy(vol_hbm, vol, small_sem.at[1])
    den_copy = pltpu.make_async_copy(den_hbm, den, small_sem.at[2])
    met_copy = pltpu.make_async_copy(met_hbm, met, small_sem.at[3])
    ids_copy = pltpu.make_async_copy(ids_hbm, ids, small_sem.at[4])

    def adj_copy(x):
        return pltpu.make_async_copy(adj_hbm.at[:, x], adj.at[:, x], in_sem.at[x])

    def vel_copy(x):
        return pltpu.make_async_copy(vel_hbm.at[:, x], vel.at[:, x], vel_sem.at[x])

    vol_copy.start()
    trace_copy.start()
    adj_copy(0).start()
    met_copy.start()
    den_copy.start()
    adj_copy(cx - 1).start()
    ids_copy.start()
    for x in range(1, cx - 1):
        adj_copy(x).start()
    for x in range(cx):
        vel_copy(x * (cx - 1) % cx).start()
    if remote:
        lax.fori_loop(1, n_span, greet_span, 0)
        lax.fori_loop(1, n_stream, greet_stream, 0)

    vol_copy.wait()
    weights[0:192, :] = vol[...].T
    trace_copy.wait()
    met_copy.wait()
    den_copy.wait()
    ids_copy.wait()

    if remote:
        left, right = lax.rem(stream + n_stream - 1, n_stream), lax.rem(stream + 1, n_stream)
        x_down = pltpu.make_async_remote_copy(
            src_ref=tx1.at[0], dst_ref=tx1.at[cx], send_sem=halo_send.at[0], recv_sem=halo_recv.at[0],
            device_id=(left, span), device_id_type=MESH)
        x_up = pltpu.make_async_remote_copy(
            src_ref=tx0.at[cx], dst_ref=tx0.at[0], send_sem=halo_send.at[1], recv_sem=halo_recv.at[1],
            device_id=(right, span), device_id_type=MESH)
        below, above = jnp.maximum(span - 1, 0), jnp.minimum(span + 1, n_span - 1)
        y_down = pltpu.make_async_remote_copy(
            src_ref=ty3.at[:, :, pl.ds(0, 128)], dst_ref=ty3.at[:, :, pl.ds(2048, 128)],
            send_sem=halo_send.at[2], recv_sem=halo_recv.at[2],
            device_id=(stream, below), device_id_type=MESH)
        y_up = pltpu.make_async_remote_copy(
            src_ref=ty2.at[:, :, pl.ds(2048, 128)], dst_ref=ty2.at[:, :, pl.ds(0, 128)],
            send_sem=halo_send.at[3], recv_sem=halo_recv.at[3],
            device_id=(stream, above), device_id_type=MESH)
        s_down = pltpu.make_async_remote_copy(
            src_ref=sens.at[0], dst_ref=sx_hi, send_sem=halo_send.at[4], recv_sem=halo_recv.at[4],
            device_id=(left, span), device_id_type=MESH)
        s_up = pltpu.make_async_remote_copy(
            src_ref=sens.at[cx - 1], dst_ref=sx_lo, send_sem=halo_send.at[5], recv_sem=halo_recv.at[5],
            device_id=(right, span), device_id_type=MESH)
        q_down = pltpu.make_async_remote_copy(
            src_ref=send_lo, dst_ref=sy_hi, send_sem=halo_send.at[6], recv_sem=halo_recv.at[6],
            device_id=(stream, below), device_id_type=MESH)
        q_up = pltpu.make_async_remote_copy(
            src_ref=send_hi, dst_ref=sy_lo, send_sem=halo_send.at[7], recv_sem=halo_recv.at[7],
            device_id=(stream, above), device_id_type=MESH)

        def a_copy(d):
            other = lax.rem(span + d, n_span)
            return pltpu.make_async_remote_copy(
                src_ref=part_a, dst_ref=slots_a.at[span], send_sem=a_send.at[d], recv_sem=a_recv.at[span],
                device_id=(stream, other), device_id_type=MESH)

        def b_copy(d):
            other = lax.rem(stream + d, n_stream)
            return pltpu.make_async_remote_copy(
                src_ref=part_b, dst_ref=slots_b.at[stream], send_sem=b_send.at[d], recv_sem=b_recv.at[stream],
                device_id=(other, span), device_id_type=MESH)

        def a_from(d):
            other = lax.rem(span + d, n_span)
            return pltpu.make_async_remote_copy(
                src_ref=part_a, dst_ref=slots_a.at[other], send_sem=a_send.at[d], recv_sem=a_recv.at[other],
                device_id=(stream, other), device_id_type=MESH)

        def b_from(d):
            other = lax.rem(stream + d, n_stream)
            return pltpu.make_async_remote_copy(
                src_ref=part_b, dst_ref=slots_b.at[other], send_sem=b_send.at[d], recv_sem=b_recv.at[other],
                device_id=(other, span), device_id_type=MESH)

    weighted = den[...] * met[...]
    lane = lax.broadcasted_iota(jnp.int32, (1, 128), 1)
    row = jnp.zeros((1, 128), F32)
    for g in range(GROUPS):
        mine = jnp.sum(jnp.where(ids[...] == g + 1, weighted, 0.0), axis=0)
        mine = jnp.sum(jnp.sum(mine, axis=0, keepdims=True), axis=1, keepdims=True)
        row = row + jnp.where(lane == g, mine, 0.0)
    part_a[...] = row
    if remote:
        slots_a[span] = row

    def slab(i, _):
        x = lax.rem(i * (cx - 1), cx)
        adj_copy(x).wait()
        rho, scale = den[x], met[x]
        alpha = 2.0 * (1.0 - rho) / (1.0 + rho)
        for y0 in range(0, 16, CHUNK):
            turned = jnp.swapaxes(adj[:, x], 0, 1)
            cols = jnp.concatenate([turned[y0 + j] for j in range(CHUNK)], axis=1)
            got = jnp.dot(weights[...], cols, preferred_element_type=F32)
            for j in range(CHUNK):
                y = y0 + j
                own = turned[y].astype(F32)
                total = got[0:192, j * 128 : (j + 1) * 128]
                base[x, y] = scale[y : y + 1] * (total + alpha[y : y + 1] * own)
            t = got[192:480]
            lanes = slice(y0 * 128, (y0 + CHUNK) * 128)
            later = slice(y0 * 128 + 128, (y0 + CHUNK) * 128 + 128)
            tx0[x + 1, :, lanes] = t[0:48].astype(BF16)
            tx1[x, :, lanes] = t[48:96].astype(BF16)
            ty2[x, :, later] = t[96:144].astype(BF16)
            ty3[x, :, lanes] = t[144:192].astype(BF16)
            for j in range(CHUNK):
                at = slice((y0 + j) * 128, (y0 + j + 1) * 128)
                tz4[x, :, at] = shift_lanes(t[192:240, j * 128 : (j + 1) * 128], False).astype(BF16)
                tz5[x, :, at] = shift_lanes(t[240:288, j * 128 : (j + 1) * 128], True).astype(BF16)

        if remote:
            @pl.when(i == 0)
            def _():
                pl.semaphore_wait(barrier, n_span + n_stream - 2)
                x_down.start()

            @pl.when(i == 1)
            def _():
                x_up.start()

        return 0

    lax.fori_loop(0, cx, slab, 0)
    if remote:
        @pl.when(span > 0)
        def _():
            y_down.start()

        @pl.when(span < n_span - 1)
        def _():
            y_up.start()

        def send_a(d, _):
            a_copy(d).start()
            return 0

        lax.fori_loop(1, n_span, send_a, 0)

    def sensing(i, _):
        x = lax.rem(i * (cx - 1), cx)
        vel_copy(x).wait()
        inner = jnp.zeros((16, 128), F32)
        for c in range(0, 192, 16):
            inner = inner + jnp.sum(adj[c : c + 16, x].astype(F32) * vel[c : c + 16, x].astype(F32), axis=0)
        rho, scale = den[x], met[x]
        slope = -4.0 / ((1.0 + rho) * (1.0 + rho))
        live = jnp.where(ids[x] > 0, 1.0, 0.0)
        value = (live * slope * scale * inner * SENS_SCALE).astype(BF16).astype(F32)
        sens[x] = value
        send_lo[pl.ds(x, 1)] = value[0:1]
        send_hi[pl.ds(x, 1)] = value[15:16]
        return 0

    lax.fori_loop(0, cx, sensing, 0)

    if remote:
        s_down.start()
        s_up.start()

        @pl.when(span > 0)
        def _():
            q_down.start()

        @pl.when(span < n_span - 1)
        def _():
            q_up.start()

        def got_a(d, _):
            a_from(d).wait_recv()
            return 0

        lax.fori_loop(1, n_span, got_a, 0)
        total = slots_a[0]
        for s in range(1, n_span):
            total = total + slots_a[s]
        part_b[...] = total
        slots_b[stream] = total

        def send_b(d, _):
            b_copy(d).start()
            return 0

        lax.fori_loop(1, n_stream, send_b, 0)

    @pl.when(span == 0)
    def _():
        for x in range(cx):
            ty2[x, :, 0:128] = jnp.zeros((ROWS, 128), BF16)
        sy_lo[...] = jnp.zeros_like(sy_lo)

    @pl.when(span == n_span - 1)
    def _():
        for x in range(cx):
            ty3[x, :, 2048:2176] = jnp.zeros((ROWS, 128), BF16)
        sy_hi[...] = jnp.zeros_like(sy_hi)

    if remote:
        def got_b(d, _):
            b_from(d).wait_recv()
            return 0

        lax.fori_loop(1, n_stream, got_b, 0)
        volumes = slots_b[0]
        for s in range(1, n_stream):
            volumes = volumes + slots_b[s]
        vol_out[...] = volumes * (1.0 / (den.shape[0] * den.shape[1] * den.shape[2]))

        def sent_a(d, _):
            a_copy(d).wait_send()
            return 0

        def sent_b(d, _):
            b_copy(d).wait_send()
            return 0

        lax.fori_loop(1, n_span, sent_a, 0)
        lax.fori_loop(1, n_stream, sent_b, 0)

        @pl.when(span > 0)
        def _():
            y_down.wait_send()
            q_down.wait_send()
            y_up.wait_recv()
            q_up.wait_recv()

        @pl.when(span < n_span - 1)
        def _():
            y_up.wait_send()
            q_up.wait_send()
            y_down.wait_recv()
            q_down.wait_recv()

        s_down.wait()
        s_up.wait()
        x_down.wait()
        x_up.wait()
    else:
        vol_out[...] = part_a[...]
        for r in (sx_lo, sx_hi, sy_lo, sy_hi):
            r[...] = jnp.zeros_like(r)


def second_kernel(
    orient_hbm, lift_hbm, base, tx0, tx1, ty2, ty3, tz4, tz5, sens, sx_lo, sx_hi, sy_lo, sy_hi, vol_in,
    res_hbm, filt, vol_out,
    orient, lift, weights, sign, turned, held, in_sem, out_sem,
):
    cx = orient.shape[1]
    orient_copy = pltpu.make_async_copy(orient_hbm, orient, in_sem.at[0])
    lift_copy = pltpu.make_async_copy(lift_hbm, lift, in_sem.at[1])
    orient_copy.start()
    lift_copy.start()

    for x in range(cx):
        own = sens[x]
        below_x = sx_lo[...] if x == 0 else sens[x - 1]
        above_x = sx_hi[...] if x == cx - 1 else sens[x + 1]
        beside = below_x + above_x
        beside = beside + shift_rows(own, sy_lo[x : x + 1], False) + shift_rows(own, sy_hi[x : x + 1], True)
        beside = beside + shift_lanes(own, False) + shift_lanes(own, True)
        filt[x] = (own + FILTER_BETA * beside) / (1.0 + 6.0 * FILTER_BETA)
    for g in range(GROUPS):
        vol_out[g] = vol_in[0, g]

    lift_copy.wait()
    weights[...] = lift[...].T
    orient_copy.wait()
    sign[...] = 1.0 - 2.0 * orient[...].astype(F32)

    def res_copy(x):
        return pltpu.make_async_copy(held.at[x], res_hbm.at[:, x], out_sem.at[x])

    def slab(x, _):
        for y0 in range(0, 16, CHUNK):
            lanes = slice(y0 * 128, (y0 + CHUNK) * 128)
            later = slice(y0 * 128 + 128, (y0 + CHUNK) * 128 + 128)
            faces = (tx0[x, :, lanes], tx1[x + 1, :, lanes], ty2[x, :, lanes], ty3[x, :, later], tz4[x, :, lanes], tz5[x, :, lanes])
            parts = []
            for k in range(6):
                rows = [jnp.broadcast_to(sign[k, x, y0 + j : y0 + j + 1], (ROWS, 128)) for j in range(CHUNK)]
                parts.append(faces[k] * jnp.concatenate(rows, axis=1).astype(BF16))
            lifted = jnp.dot(weights[...], jnp.concatenate(parts, axis=0), preferred_element_type=F32)
            for j in range(CHUNK):
                turned[y0 + j] = (base[x, y0 + j] + lifted[:, j * 128 : (j + 1) * 128]).astype(BF16)
        held[x] = jnp.swapaxes(turned[...], 0, 1)
        res_copy(x).start()
        return 0

    lax.fori_loop(0, cx, slab, 0)
    for x in range(cx):
        res_copy(x).wait()


def in_hbm(array):
    return pltpu.with_memory_space_constraint(array, pltpu.HBM)


def shards(
    n_stream, n_span, remote,
    adjoint, velocity, density, metric, orientation, design_ids, volume_block, face_trace, face_lift
):
    cx = adjoint.shape[1]
    any_spec = pl.BlockSpec(memory_space=pltpu.HBM)
    vmem_spec = pl.BlockSpec(memory_space=pltpu.VMEM)
    mids = [
        ((cx, 16, 192, 128), F32),
        ((cx + 1, ROWS, 2048), BF16),
        ((cx + 1, ROWS, 2048), BF16),
        ((cx, ROWS, 2176), BF16),
        ((cx, ROWS, 2176), BF16),
        ((cx, ROWS, 2048), BF16),
        ((cx, ROWS, 2048), BF16),
        ((cx, 16, 128), F32),
        ((16, 128), F32),
        ((16, 128), F32),
        ((8, 128), F32),
        ((8, 128), F32),
        ((1, 128), F32),
    ]
    dma = pltpu.SemaphoreType.DMA
    whole = (adjoint, velocity, density, metric, design_ids, volume_block, face_trace.reshape(288, 192))
    lift_rows = jnp.swapaxes(face_lift, 1, 2).reshape(288, 192)
    whole, (orientation, lift_rows) = jax.tree.map(in_hbm, (whole, (orientation, lift_rows)))
    mid = pl.pallas_call(
        functools.partial(first_kernel, n_stream, n_span, remote),
        out_shape=[pltpu.VMEM(s, d) for s, d in mids],
        in_specs=[any_spec] * 7,
        out_specs=[vmem_spec] * len(mids),
        scratch_shapes=[
            pltpu.VMEM((192, cx, 16, 128), BF16),
            pltpu.VMEM((192, cx, 16, 128), BF16),
            pltpu.VMEM((cx, 16, 128), F32),
            pltpu.VMEM((cx, 16, 128), F32),
            pltpu.VMEM((cx, 16, 128), jnp.int32),
            pltpu.VMEM((192, 192), BF16),
            pltpu.VMEM((480, 192), BF16),
            pltpu.VMEM((8, 128), F32),
            pltpu.VMEM((8, 128), F32),
            pltpu.VMEM((n_span, 1, 128), F32),
            pltpu.VMEM((n_stream, 1, 128), F32),
            pltpu.VMEM((1, 128), F32),
            pltpu.VMEM((1, 128), F32),
            dma((cx,)), dma((cx,)), dma((5,)), dma((8,)), dma((8,)),
            dma((n_span,)), dma((n_span,)), dma((n_stream,)), dma((n_stream,)),
        ],
        compiler_params=pltpu.CompilerParams(
            collective_id=0 if remote else None, has_side_effects=True, vmem_limit_bytes=24 * 2**20
        ),
    )(*whole)
    mid = [pltpu.with_memory_space_constraint(m, pltpu.VMEM) for m in mid]
    return pl.pallas_call(
        second_kernel,
        out_shape=[
            jax.ShapeDtypeStruct(adjoint.shape, BF16),
            jax.ShapeDtypeStruct((cx, 16, 128), F32),
            jax.ShapeDtypeStruct((GROUPS,), F32),
        ],
        in_specs=[any_spec] * 2 + [vmem_spec] * len(mids),
        out_specs=[any_spec, vmem_spec, pl.BlockSpec(memory_space=pltpu.SMEM)],
        scratch_shapes=[
            pltpu.VMEM((6, cx, 16, 128), jnp.int32),
            pltpu.VMEM((288, 192), BF16),
            pltpu.VMEM((192, 288), BF16),
            pltpu.VMEM((6, cx, 16, 128), F32),
            pltpu.VMEM((16, 192, 128), BF16),
            pltpu.VMEM((cx, 192, 16, 128), BF16),
            dma((2,)), dma((cx,)),
        ],
        compiler_params=pltpu.CompilerParams(vmem_limit_bytes=24 * 2**20),
    )(orientation, lift_rows, *mid)


def solution(mesh, remote=True):
    cells = P("stream", "span", None)
    dofs = P(None, "stream", "span", None)
    return jax.shard_map(
        functools.partial(shards, mesh.shape["stream"], mesh.shape["span"], remote),
        mesh=mesh,
        in_specs=(dofs, dofs, cells, cells, dofs, cells, P(), P(), P()),
        out_specs=(dofs, cells, P()),
        check_vma=False,
    )
```

time: 180 us -> 35.7 us (0.20)
  blocking collectives: 83.9 us -> 0 us
  matrix products: 44.5 us -> 0 us
  Pallas kernels: 0 us -> 34.9 us
  starting transfers between devices: 16.6 us -> 0 us
  local copies, waits for them, and re-layouts: 14.6 us -> 0 us
  waiting for transfers between devices: 10.5 us -> 0 us
  other arithmetic: 8.65 us -> 0 us
    psum x1 -> x0, blocking collectives: 83.9 us -> none  [shards(): lax.psum(partial_value, ('stream', 'span')) / jnp.float32(density.size)]
    dot_general x12 -> x0, matrix products: 44.5 us -> none  [the longest x6 22.1 us: shards(): jnp.einsum('jt,txyz->jxyz', face_lift[face], neighbours[face], preferred_...]
    pallas_call x0 -> x2, Pallas kernels: none -> 34.9 us  [the longest x1 28.9 us: shards(): pl.pallas_call(functools.partial(first_kernel, n_stream, n_span, remote),...]
    ppermute x8 -> x0, starting transfers between devices: 16.6 us -> none  [the longest x4 9.89 us: extended(): lax.ppermute(tail, axis, [(i, (i + 1) % count) for i in range(ends)])]
    ppermute x8 -> x0, waiting for transfers between devices: 10.5 us -> none  [the longest x4 10.5 us: extended(): lax.ppermute(head, axis, [((i + 1) % count, i) for i in range(ends)])]
    unnamed x39 -> x0, local copies, waits for them, and re-layouts: 6.82 us -> none
    slice x12 -> x0, local copies, waits for them, and re-layouts: 5.83 us -> none  [the longest x1 1.49 us: shards(): stream_send = edge_pair(adjoint[:, :1], adjoint[:, -1:], 1)]
    dot_general x1 -> x0, other arithmetic: 4.29 us -> none  [shards(): jnp.einsum('ixyz,ixyz->xyz', velocity, adjoint, preferred_element_type=jn...]
  transfers between devices with their start and end apart: 8 -> 0, of which waited for: 1 -> 0; matrix products, arithmetic and copies ran while one was open for 19% -> 0% of each run, Pallas kernels for 0% -> 0%
where the time goes in v1:
time: 35.7 us; the launch traced here: 35.6 us
  Pallas kernels  34.9 us (98%)
  between operations  0.64 us (2%)
    pallas_call x1, Pallas kernels, shards(): pl.pallas_call(functools.partial(first_kernel, n_stream, n_span, remote),...  28.9 us
    pallas_call x1, Pallas kernels, shards(): pl.pallas_call(second_kernel, out_shape=[jax.ShapeDtypeStruct(adjoint.sha...  6 us

profile of v1, /device:TPU:1, one launch (start us, length us, event | category | flops | bytes accessed | tf_op | source)
XLA Modules:
  0.0 35.6 jit_solution(362668150139984589)
XLA Ops:
  0.6 28.9 %shard_map.112 = (f32[4,16,192,128]{3,2,1,0:T(8,128)S(1)}, bf16[5,48,2048]{2,1,0:T(8,128)(2,1)S(1)}, bf16[5,48,2048]{2,1,0:T(8,128)(2,1)S(1)}, bf16[4,48,2176]{2...) custom-call(bf16[192,4,16,128]{3,2,1,0:T(8,128)(2,1)} %adj_hbm.1, ...), custom_call_target="tpu_custom_call" | custom-call | tf_op jit(solution)/shard_map/pallas_call | solution.py:393
  29.6 6.0 %shard_map.113 = (bf16[192,4,16,128]{3,2,1,0:T(8,128)(2,1)}, f32[4,16,128]{2,1,0:T(8,128)}, f32[4]{0:T(128)}) custom-call(s32[6,4,16,128]{3,2,1,0:T(8,128)} %orient_hbm.1, bf16[288,192]{1,0:T(8,128)(2,1)} %bitcast.5, f32[4,16,192,128]{3,2,1,0:T(8,128)S(1)} %get-tuple-element.16.base, bf16[5,48,2048]{2,1,0:T(8,128)(2,1)S(1)} %get-tuple-element.17.tx0, ...), custom_call_target="tpu_custom_call" | custom-call | tf_op jit(solution)/shard_map/pallas_call | solution.py:420

commit v2 on v1

v2 whole, which is shorter than its diff:
```python
import functools

import jax
import jax.numpy as jnp
from jax import lax
from jax.experimental import pallas as pl
from jax.experimental.pallas import tpu as pltpu
from jax.sharding import PartitionSpec as P

MESH = pl.DeviceIdType.MESH
F32 = jnp.float32
BF16 = jnp.bfloat16
GROUPS = 4
SENS_SCALE = 0.03125
FILTER_BETA = 0.5
ROWS = 48
CHUNK = 4
PLANE = 4


def shift_rows(field, first, up):
    row = lax.broadcasted_iota(jnp.int32, field.shape, 0)
    edge = field.shape[0] - 1 if up else 0
    moved = pltpu.roll(field, field.shape[0] - 1 if up else 1, 0)
    return jnp.where(row == edge, first, moved)


def shift_lanes(field, up):
    lane = lax.broadcasted_iota(jnp.int32, field.shape, field.ndim - 1)
    edge = 127 if up else 0
    moved = pltpu.roll(field, 127 if up else 1, field.ndim - 1)
    return jnp.where(lane == edge, jnp.zeros_like(field), moved)


def wait_for_copies(slots, count, send_sem, recv_sem, device):
    return pltpu.make_async_remote_copy(
        src_ref=slots.at[pl.ds(0, count)], dst_ref=slots.at[pl.ds(0, count)],
        send_sem=send_sem, recv_sem=recv_sem, device_id=device, device_id_type=MESH)


def first_kernel(
    n_stream, n_span, remote,
    adj_hbm, vel_hbm, den_hbm, met_hbm, ids_hbm, orient_hbm, vol_hbm, trace_hbm, lift_hbm,
    held, filt, vol_out,
    adj, vel, den, met, ids, orient, vol, lift, weights, lift_weights, sign, turned, back, base,
    tx0, tx1, ty2, ty3, tz4, tz5, sens, sx_lo, sx_hi, sy_lo, sy_hi,
    send_lo, send_hi, slots_a, slots_b, part_a, part_b,
    in_sem, vel_sem, small_sem, halo_send, halo_recv, vol_send, vol_recv,
):
    cx = adj.shape[1]
    stream, span = lax.axis_index("stream"), lax.axis_index("span")
    left, right = lax.rem(stream + n_stream - 1, n_stream), lax.rem(stream + 1, n_stream)
    below, above = jnp.maximum(span - 1, 0), jnp.minimum(span + 1, n_span - 1)
    n_plane = PLANE * n_span
    n_line = n_stream // PLANE
    line, seat = stream // PLANE, lax.rem(stream, PLANE)
    spot = seat * n_span + span

    def in_plane(d):
        other = lax.rem(spot + d, n_plane)
        return (line * PLANE + other // n_span, lax.rem(other, n_span))

    def in_line(d):
        return (lax.rem(line + d, n_line) * PLANE + seat, span)

    def adj_copy(x):
        return pltpu.make_async_copy(adj_hbm.at[:, x], adj.at[:, x], in_sem.at[x])

    def vel_copy(x):
        return pltpu.make_async_copy(vel_hbm.at[:, x], vel.at[:, x], vel_sem.at[x])

    small = [
        pltpu.make_async_copy(a, b, small_sem.at[i])
        for i, (a, b) in enumerate((
            (vol_hbm, vol), (trace_hbm, weights.at[pl.ds(192, 288)]), (den_hbm, den), (met_hbm, met),
            (ids_hbm, ids), (orient_hbm, orient), (lift_hbm, lift)))
    ]
    for c in small[:5]:
        c.start()
    adj_copy(0).start()
    adj_copy(cx - 1).start()
    vel_copy(0).start()
    adj_copy(2).start()
    vel_copy(cx - 1).start()
    adj_copy(1).start()
    vel_copy(2).start()
    vel_copy(1).start()
    for c in small[5:]:
        c.start()

    if remote:
        barrier = pltpu.get_barrier_semaphore()

        def greet(device):
            pl.semaphore_signal(barrier, inc=1, device_id=device, device_id_type=MESH)

        def greet_plane(d, _):
            greet(in_plane(d))
            return 0

        def greet_line(d, _):
            greet(in_line(d))
            return 0

        greet((left, span))
        greet((right, span))
        lax.fori_loop(1, n_plane, greet_plane, 0)
        lax.fori_loop(1, n_line, greet_line, 0)

        def halo(i, src, dst, device):
            return pltpu.make_async_remote_copy(
                src_ref=src, dst_ref=dst, send_sem=halo_send.at[i], recv_sem=halo_recv.at[i],
                device_id=device, device_id_type=MESH)

        x_down = halo(0, tx1.at[0], tx1.at[cx], (left, span))
        x_up = halo(1, tx0.at[cx], tx0.at[0], (right, span))
        y_down = halo(2, ty3.at[:, :, pl.ds(0, 128)], ty3.at[:, :, pl.ds(2048, 128)], (stream, below))
        y_up = halo(3, ty2.at[:, :, pl.ds(2048, 128)], ty2.at[:, :, pl.ds(0, 128)], (stream, above))
        s_down = halo(4, sens.at[0], sx_hi, (left, span))
        s_up = halo(5, sens.at[cx - 1], sx_lo, (right, span))
        q_down = halo(6, send_lo, sy_hi, (stream, below))
        q_up = halo(7, send_hi, sy_lo, (stream, above))

        def send_a(d, _):
            pltpu.make_async_remote_copy(
                src_ref=part_a, dst_ref=slots_a.at[spot], send_sem=vol_send.at[0], recv_sem=vol_recv.at[0],
                device_id=in_plane(d), device_id_type=MESH).start()
            return 0

        def send_b(d, _):
            pltpu.make_async_remote_copy(
                src_ref=part_b, dst_ref=slots_b.at[line], send_sem=vol_send.at[1], recv_sem=vol_recv.at[1],
                device_id=in_line(d), device_id_type=MESH).start()
            return 0

        all_a = wait_for_copies(slots_a, n_plane - 1, vol_send.at[0], vol_recv.at[0], in_plane(1))
        all_b = wait_for_copies(slots_b, n_line - 1, vol_send.at[1], vol_recv.at[1], in_line(1))

    def turn(x):
        for d in range(0, 192, 16):
            turned[x, :, d : d + 16] = jnp.swapaxes(adj[d : d + 16, x], 0, 1)

    def sense(x):
        inner = jnp.zeros((16, 128), F32)
        for c in range(0, 192, 16):
            inner = inner + jnp.sum(adj[c : c + 16, x].astype(F32) * vel[c : c + 16, x].astype(F32), axis=0)
        rho, scale = den[x], met[x]
        slope = -4.0 / ((1.0 + rho) * (1.0 + rho))
        live = jnp.where(ids[x] > 0, 1.0, 0.0)
        value = (live * slope * scale * inner * SENS_SCALE).astype(BF16).astype(F32)
        sens[x] = value
        send_lo[pl.ds(x, 1)] = value[0:1]
        send_hi[pl.ds(x, 1)] = value[15:16]

    def traces(x):
        rho, scale = den[x], met[x]
        alpha = 2.0 * (1.0 - rho) / (1.0 + rho)
        for y0 in range(0, 16, CHUNK):
            cols = jnp.concatenate([turned[x, y0 + j] for j in range(CHUNK)], axis=1)
            got = jnp.dot(weights[...], cols, preferred_element_type=F32)
            for j in range(CHUNK):
                y = y0 + j
                own = turned[x, y].astype(F32)
                total = got[0:192, j * 128 : (j + 1) * 128]
                base[x, y] = scale[y : y + 1] * (total + alpha[y : y + 1] * own)
            t = got[192:480]
            lanes = slice(y0 * 128, (y0 + CHUNK) * 128)
            later = slice(y0 * 128 + 128, (y0 + CHUNK) * 128 + 128)
            tx0[x + 1, :, lanes] = t[0:48].astype(BF16)
            tx1[x, :, lanes] = t[48:96].astype(BF16)
            ty2[x, :, later] = t[96:144].astype(BF16)
            ty3[x, :, lanes] = t[144:192].astype(BF16)
            for j in range(CHUNK):
                at = slice((y0 + j) * 128, (y0 + j + 1) * 128)
                tz4[x, :, at] = shift_lanes(t[192:240, j * 128 : (j + 1) * 128], False).astype(BF16)
                tz5[x, :, at] = shift_lanes(t[240:288, j * 128 : (j + 1) * 128], True).astype(BF16)

    def order(i):
        return lax.rem(i * (cx - 1), cx)

    def slab(i, _):
        x, ahead = order(i), order(i + 1)

        @pl.when(i < cx - 1)
        def _():
            adj_copy(ahead).wait()

        vel_copy(x).wait()
        traces(x)
        sense(x)
        turn(ahead)
        if remote:
            @pl.when(i == 0)
            def _():
                pl.semaphore_wait(barrier, n_plane + n_line)
                lax.fori_loop(1, n_plane, send_a, 0)
                x_down.start()

            @pl.when(i == 1)
            def _():
                x_up.start()

        return 0

    for c in small[:5]:
        c.wait()
    weights[0:192, :] = vol[...].T

    weighted = den[...] * met[...]
    lane = lax.broadcasted_iota(jnp.int32, (1, 128), 1)
    row = jnp.zeros((1, 128), F32)
    for g in range(GROUPS):
        mine = jnp.sum(jnp.where(ids[...] == g + 1, weighted, 0.0), axis=0)
        mine = jnp.sum(jnp.sum(mine, axis=0, keepdims=True), axis=1, keepdims=True)
        row = row + jnp.where(lane == g, mine, 0.0)
    part_a[...] = row
    if remote:
        slots_a[spot] = row

    adj_copy(0).wait()
    turn(0)
    lax.fori_loop(0, cx, slab, 0)
    if remote:
        @pl.when(span > 0)
        def _():
            y_down.start()
            q_down.start()

        @pl.when(span < n_span - 1)
        def _():
            y_up.start()
            q_up.start()

        s_down.start()
        s_up.start()

    small[6].wait()
    lift_weights[...] = lift[...].T
    small[5].wait()
    sign[...] = 1.0 - 2.0 * orient[...].astype(F32)

    if remote:
        all_a.wait_recv()
        total = slots_a[0]
        for s in range(1, n_plane):
            total = total + slots_a[s]
        part_b[...] = total
        slots_b[line] = total
        lax.fori_loop(1, n_line, send_b, 0)

    @pl.when(span == 0)
    def _():
        for x in range(cx):
            ty2[x, :, 0:128] = jnp.zeros((ROWS, 128), BF16)
        sy_lo[...] = jnp.zeros_like(sy_lo)

    @pl.when(span == n_span - 1)
    def _():
        for x in range(cx):
            ty3[x, :, 2048:2176] = jnp.zeros((ROWS, 128), BF16)
        sy_hi[...] = jnp.zeros_like(sy_hi)

    if remote:
        @pl.when(span > 0)
        def _():
            y_up.wait_recv()

        @pl.when(span < n_span - 1)
        def _():
            y_down.wait_recv()

    def lifted(x):
        for y0 in range(0, 16, CHUNK):
            lanes = slice(y0 * 128, (y0 + CHUNK) * 128)
            later = slice(y0 * 128 + 128, (y0 + CHUNK) * 128 + 128)
            faces = (tx0[x, :, lanes], tx1[x + 1, :, lanes], ty2[x, :, lanes], ty3[x, :, later], tz4[x, :, lanes], tz5[x, :, lanes])
            parts = []
            for k in range(6):
                rows = [jnp.broadcast_to(sign[k, x, y0 + j : y0 + j + 1], (ROWS, 128)) for j in range(CHUNK)]
                parts.append(faces[k] * jnp.concatenate(rows, axis=1).astype(BF16))
            got = jnp.dot(lift_weights[...], jnp.concatenate(parts, axis=0), preferred_element_type=F32)
            for j in range(CHUNK):
                back[x, y0 + j] = (base[x, y0 + j] + got[:, j * 128 : (j + 1) * 128]).astype(BF16)

    def turn_back(x):
        for d in range(0, 192, 16):
            held[d : d + 16, x] = jnp.swapaxes(back[x, :, d : d + 16], 0, 1)

    def late(i):
        return jnp.where(i < 2, i + 1, (cx - 1) * (i - 2))

    def finish(i, _):
        if remote:
            @pl.when(i == 2)
            def _():
                x_down.wait_recv()
                x_up.wait_recv()

        x = late(i)
        before = late(jnp.maximum(i - 1, 0))
        lifted(x)
        turn_back(before)
        return 0

    lax.fori_loop(0, cx, finish, 0)
    turn_back(late(cx - 1))

    if remote:
        @pl.when(span > 0)
        def _():
            y_down.wait_send()
            q_down.wait_send()
            q_up.wait_recv()

        @pl.when(span < n_span - 1)
        def _():
            y_up.wait_send()
            q_up.wait_send()
            q_down.wait_recv()

        s_down.wait()
        s_up.wait()
        x_down.wait_send()
        x_up.wait_send()
    else:
        for r in (sx_lo, sx_hi, sy_lo, sy_hi):
            r[...] = jnp.zeros_like(r)

    for x in range(cx):
        own = sens[x]
        below_x = sx_lo[...] if x == 0 else sens[x - 1]
        above_x = sx_hi[...] if x == cx - 1 else sens[x + 1]
        beside = below_x + above_x
        beside = beside + shift_rows(own, sy_lo[x : x + 1], False) + shift_rows(own, sy_hi[x : x + 1], True)
        beside = beside + shift_lanes(own, False) + shift_lanes(own, True)
        filt[x] = (own + FILTER_BETA * beside) / (1.0 + 6.0 * FILTER_BETA)

    if remote:
        all_b.wait_recv()
        volumes = slots_b[0]
        for s in range(1, n_line):
            volumes = volumes + slots_b[s]
        vol_out[...] = volumes * (1.0 / (den.shape[0] * den.shape[1] * den.shape[2]))
        all_a.wait_send()
        all_b.wait_send()
    else:
        vol_out[...] = part_a[...]


def second_kernel(held, filt_in, vol_in, res_hbm, filt, vol_out, out_sem):
    pieces = out_sem.shape[0]
    step = held.shape[0] // pieces
    copies = [
        pltpu.make_async_copy(held.at[pl.ds(i * step, step)], res_hbm.at[pl.ds(i * step, step)], out_sem.at[i])
        for i in range(pieces)
    ]
    for c in copies:
        c.start()
    filt[...] = filt_in[...]
    for g in range(GROUPS):
        vol_out[g] = vol_in[0, g]
    for c in copies:
        c.wait()


def in_hbm(array):
    return pltpu.with_memory_space_constraint(array, pltpu.HBM)


def shards(
    n_stream, n_span, remote,
    adjoint, velocity, density, metric, orientation, design_ids, volume_block, face_trace, face_lift
):
    cx = adjoint.shape[1]
    hbm_spec = pl.BlockSpec(memory_space=pltpu.HBM)
    vmem_spec = pl.BlockSpec(memory_space=pltpu.VMEM)
    dma = pltpu.SemaphoreType.DMA
    lift_rows = jnp.swapaxes(face_lift, 1, 2).reshape(288, 192)
    whole = (adjoint, velocity, density, metric, design_ids, orientation, volume_block, face_trace.reshape(288, 192), lift_rows)
    cells = (cx, 16, 128)
    dofs = (192, cx, 16, 128)
    mids = [(dofs, BF16), (cells, F32), ((1, 128), F32)]
    n_plane, n_line = PLANE * n_span, n_stream // PLANE
    mid = pl.pallas_call(
        functools.partial(first_kernel, n_stream, n_span, remote),
        out_shape=[pltpu.VMEM(s, d) for s, d in mids],
        in_specs=[hbm_spec] * len(whole),
        out_specs=[vmem_spec] * len(mids),
        scratch_shapes=[
            pltpu.VMEM(dofs, BF16),
            pltpu.VMEM(dofs, BF16),
            pltpu.VMEM(cells, F32),
            pltpu.VMEM(cells, F32),
            pltpu.VMEM(cells, jnp.int32),
            pltpu.VMEM((6, *cells), jnp.int32),
            pltpu.VMEM((192, 192), BF16),
            pltpu.VMEM((288, 192), BF16),
            pltpu.VMEM((480, 192), BF16),
            pltpu.VMEM((192, 288), BF16),
            pltpu.VMEM((6, *cells), F32),
            pltpu.VMEM((cx, 16, 192, 128), BF16),
            pltpu.VMEM((cx, 16, 192, 128), BF16),
            pltpu.VMEM((cx, 16, 192, 128), F32),
            pltpu.VMEM((cx + 1, ROWS, 2048), BF16),
            pltpu.VMEM((cx + 1, ROWS, 2048), BF16),
            pltpu.VMEM((cx, ROWS, 2176), BF16),
            pltpu.VMEM((cx, ROWS, 2176), BF16),
            pltpu.VMEM((cx, ROWS, 2048), BF16),
            pltpu.VMEM((cx, ROWS, 2048), BF16),
            pltpu.VMEM(cells, F32),
            pltpu.VMEM((16, 128), F32),
            pltpu.VMEM((16, 128), F32),
            pltpu.VMEM((8, 128), F32),
            pltpu.VMEM((8, 128), F32),
            pltpu.VMEM((8, 128), F32),
            pltpu.VMEM((8, 128), F32),
            pltpu.VMEM((n_plane, 1, 128), F32),
            pltpu.VMEM((max(n_line, 1), 1, 128), F32),
            pltpu.VMEM((1, 128), F32),
            pltpu.VMEM((1, 128), F32),
            dma((cx,)), dma((cx,)), dma((7,)), dma((8,)), dma((8,)), dma((2,)), dma((2,)),
        ],
        compiler_params=pltpu.CompilerParams(
            collective_id=0 if remote else None, has_side_effects=True, vmem_limit_bytes=44 * 2**20
        ),
    )(*[in_hbm(a) for a in whole])
    return pl.pallas_call(
        second_kernel,
        out_shape=[
            jax.ShapeDtypeStruct(adjoint.shape, BF16),
            jax.ShapeDtypeStruct(cells, F32),
            jax.ShapeDtypeStruct((GROUPS,), F32),
        ],
        in_specs=[vmem_spec] * len(mids),
        out_specs=[hbm_spec, vmem_spec, pl.BlockSpec(memory_space=pltpu.SMEM)],
        scratch_shapes=[dma((8,))],
        compiler_params=pltpu.CompilerParams(vmem_limit_bytes=4 * 2**20),
    )(*[pltpu.with_memory_space_constraint(m, pltpu.VMEM) for m in mid])


def solution(mesh, remote=True):
    cells = P("stream", "span", None)
    dofs = P(None, "stream", "span", None)
    return jax.shard_map(
        functools.partial(shards, mesh.shape["stream"], mesh.shape["span"], remote),
        mesh=mesh,
        in_specs=(dofs, dofs, cells, cells, dofs, cells, P(), P(), P()),
        out_specs=(dofs, cells, P()),
        check_vma=False,
    )
```

time: 35.7 us -> 25.6 us (0.72)
  Pallas kernels: 34.9 us -> 24.9 us
    pallas_call x1, Pallas kernels: 28.9 us -> 22.6 us  [shards(): pl.pallas_call(functools.partial(first_kernel, n_stream, n_span, remote),...]
    pallas_call x1, Pallas kernels: 6 us -> 2.35 us  [shards(): pl.pallas_call(second_kernel, out_shape=[jax.ShapeDtypeStruct(adjoint.sha...]
where the time goes in v2:
time: 25.6 us
  Pallas kernels  24.9 us (97%)
  between operations  0.64 us (2%)
    pallas_call x1, Pallas kernels, shards(): pl.pallas_call(functools.partial(first_kernel, n_stream, n_span, remote),...  22.6 us
    pallas_call x1, Pallas kernels, shards(): pl.pallas_call(second_kernel, out_shape=[jax.ShapeDtypeStruct(adjoint.sha...  2.35 us

profile of v2, /device:TPU:1, one launch (start us, length us, event | category | flops | bytes accessed | tf_op | source)
XLA Modules:
  0.0 25.6 jit_solution(14656258573753894473)
XLA Ops:
  0.6 22.6 %shard_map.112 = (bf16[192,4,16,128]{3,2,1,0:T(8,128)(2,1)S(1)}, f32[4,16,128]{2,1,0:T(8,128)S(1)}, f32[1,128]{1,0:T(1,128)S(1)}) custom-call(bf16[192,4,16,128]{3,2,1,0:T(8,128)(2,1)} %adj_hbm.1, bf16[192,4,16,128]{3,2,1,0:T(8,128)(2,1)} %vel_hbm.1, f32[4,16,128]{2,1,0:T(8,128)} %den_hbm.1, f32[4,16,128]{2,1,0:T(8,128)} %met_hbm.1, s32[4,16,128]{2,1,0:T(8,128)} %ids_hbm.1, ...), custom_call_target="tpu_custom_call" | custom-call | tf_op jit(solution)/shard_map/pallas_call | solution.py:384
  23.2 2.3 %shard_map.113 = (bf16[192,4,16,128]{3,2,1,0:T(8,128)(2,1)}, f32[4,16,128]{2,1,0:T(8,128)}, f32[4]{0:T(128)}) custom-call(bf16[192,4,16,128]{3,2,1,0:T(8,128)(2,1)S(1)} %get-tuple-element.6.held, f32[4,16,128]{2,1,0:T(8,128)S(1)} %get-tuple-element.7.filt_in, f32[1,128]{1,0:T(1,128)S(1)} %get-tuple-element.8.vol_in), custom_call_target="tpu_custom_call" | custom-call | tf_op jit(solution)/shard_map/pallas_call | solution.py:427

commit v3 on v2

--- a/solution.py
+++ b/solution.py
@@ -42,12 +42,13 @@
     n_stream, n_span, remote,
     adj_hbm, vel_hbm, den_hbm, met_hbm, ids_hbm, orient_hbm, vol_hbm, trace_hbm, lift_hbm,
     held, filt, vol_out,
-    adj, vel, den, met, ids, orient, vol, lift, weights, lift_weights, sign, turned, back, base,
+    adj, vel, den, met, ids, orient, vol, lift, weights, lift_weights, sign, turned_a, turned_b, turned_c, turned_d, back_a, back_b, base,
     tx0, tx1, ty2, ty3, tz4, tz5, sens, sx_lo, sx_hi, sy_lo, sy_hi,
     send_lo, send_hi, slots_a, slots_b, part_a, part_b,
     in_sem, vel_sem, small_sem, halo_send, halo_recv, vol_send, vol_recv,
 ):
     cx = adj.shape[1]
+    turned = (turned_a, turned_b, turned_c, turned_d)
     stream, span = lax.axis_index("stream"), lax.axis_index("span")
     left, right = lax.rem(stream + n_stream - 1, n_stream), lax.rem(stream + 1, n_stream)
     below, above = jnp.maximum(span - 1, 0), jnp.minimum(span + 1, n_span - 1)
@@ -55,13 +56,10 @@
     n_line = n_stream // PLANE
     line, seat = stream // PLANE, lax.rem(stream, PLANE)
     spot = seat * n_span + span
-
-    def in_plane(d):
-        other = lax.rem(spot + d, n_plane)
-        return (line * PLANE + other // n_span, lax.rem(other, n_span))
-
-    def in_line(d):
-        return (lax.rem(line + d, n_line) * PLANE + seat, span)
+    seats = [line * PLANE + lax.rem(seat + d, PLANE) for d in range(PLANE)]
+    spans = [lax.rem(span + d, n_span) for d in range(n_span)]
+    in_plane = [(seats[d // n_span], spans[d % n_span]) for d in range(n_plane - 1, 0, -1)]
+    in_line = [(lax.rem(line + d, n_line) * PLANE + seat, span) for d in range(1, n_line)]
 
     def adj_copy(x):
         return pltpu.make_async_copy(adj_hbm.at[:, x], adj.at[:, x], in_sem.at[x])
@@ -75,18 +73,14 @@
             (vol_hbm, vol), (trace_hbm, weights.at[pl.ds(192, 288)]), (den_hbm, den), (met_hbm, met),
             (ids_hbm, ids), (orient_hbm, orient), (lift_hbm, lift)))
     ]
-    for c in small[:5]:
+    vol_copy, trace_copy, den_copy, met_copy, ids_copy, orient_copy, lift_copy = small
+    trace_copy.start()
+    adj_copy(0).start()
+    for c in (den_copy, met_copy, ids_copy):
         c.start()
-    adj_copy(0).start()
-    adj_copy(cx - 1).start()
-    vel_copy(0).start()
-    adj_copy(2).start()
-    vel_copy(cx - 1).start()
-    adj_copy(1).start()
-    vel_copy(2).start()
-    vel_copy(1).start()
-    for c in small[5:]:
-        c.start()
+    for x in (cx - 1, 2, 1):
+        adj_copy(x).start()
+    vol_copy.start()
 
     if remote:
         barrier = pltpu.get_barrier_semaphore()
@@ -94,18 +88,10 @@
         def greet(device):
             pl.semaphore_signal(barrier, inc=1, device_id=device, device_id_type=MESH)
 
-        def greet_plane(d, _):
-            greet(in_plane(d))
-            return 0
-
-        def greet_line(d, _):
-            greet(in_line(d))
-            return 0
-
         greet((left, span))
         greet((right, span))
-        lax.fori_loop(1, n_plane, greet_plane, 0)
-        lax.fori_loop(1, n_line, greet_line, 0)
+        for device in in_plane + in_line:
+            greet(device)
 
         def halo(i, src, dst, device):
             return pltpu.make_async_remote_copy(
@@ -121,24 +107,18 @@
         q_down = halo(6, send_lo, sy_hi, (stream, below))
         q_up = halo(7, send_hi, sy_lo, (stream, above))
 
-        def send_a(d, _):
-            pltpu.make_async_remote_copy(
-                src_ref=part_a, dst_ref=slots_a.at[spot], send_sem=vol_send.at[0], recv_sem=vol_recv.at[0],
-                device_id=in_plane(d), device_id_type=MESH).start()
-            return 0
-
-        def send_b(d, _):
-            pltpu.make_async_remote_copy(
-                src_ref=part_b, dst_ref=slots_b.at[line], send_sem=vol_send.at[1], recv_sem=vol_recv.at[1],
-                device_id=in_line(d), device_id_type=MESH).start()
-            return 0
-
-        all_a = wait_for_copies(slots_a, n_plane - 1, vol_send.at[0], vol_recv.at[0], in_plane(1))
-        all_b = wait_for_copies(slots_b, n_line - 1, vol_send.at[1], vol_recv.at[1], in_line(1))
-
-    def turn(x):
+        def send_to_all(devices, part, slot, i):
+            for device in devices:
+                pltpu.make_async_remote_copy(
+                    src_ref=part, dst_ref=slot, send_sem=vol_send.at[i], recv_sem=vol_recv.at[i],
+                    device_id=device, device_id_type=MESH).start()
+
+        all_a = wait_for_copies(slots_a, n_plane - 1, vol_send.at[0], vol_recv.at[0], in_plane[0])
+        all_b = wait_for_copies(slots_b, n_line - 1, vol_send.at[1], vol_recv.at[1], in_line[0])
+
+    def turn(x, to):
         for d in range(0, 192, 16):
-            turned[x, :, d : d + 16] = jnp.swapaxes(adj[d : d + 16, x], 0, 1)
+            to[:, d : d + 16] = jnp.swapaxes(adj[d : d + 16, x], 0, 1)
 
     def sense(x):
         inner = jnp.zeros((16, 128), F32)
@@ -152,59 +132,66 @@
         send_lo[pl.ds(x, 1)] = value[0:1]
         send_hi[pl.ds(x, 1)] = value[15:16]
 
-    def traces(x):
+    def traces(x, turned):
         rho, scale = den[x], met[x]
         alpha = 2.0 * (1.0 - rho) / (1.0 + rho)
         for y0 in range(0, 16, CHUNK):
-            cols = jnp.concatenate([turned[x, y0 + j] for j in range(CHUNK)], axis=1)
+            cols = jnp.concatenate([turned[y0 + j] for j in range(CHUNK)], axis=1)
             got = jnp.dot(weights[...], cols, preferred_element_type=F32)
             for j in range(CHUNK):
                 y = y0 + j
-                own = turned[x, y].astype(F32)
+                own = turned[y].astype(F32)
                 total = got[0:192, j * 128 : (j + 1) * 128]
                 base[x, y] = scale[y : y + 1] * (total + alpha[y : y + 1] * own)
             t = got[192:480]
             lanes = slice(y0 * 128, (y0 + CHUNK) * 128)
-            later = slice(y0 * 128 + 128, (y0 + CHUNK) * 128 + 128)
-            tx0[x + 1, :, lanes] = t[0:48].astype(BF16)
-            tx1[x, :, lanes] = t[48:96].astype(BF16)
-            ty2[x, :, later] = t[96:144].astype(BF16)
-            ty3[x, :, lanes] = t[144:192].astype(BF16)
+            if x < cx - 1:
+                tx0[x + 1, :, lanes] = t[0:48].astype(BF16)
+            if x > 0:
+                tx1[x, :, lanes] = t[48:96].astype(BF16)
+            top = min(y0 + CHUNK, 15) - y0
+            ty2[x, :, y0 * 128 + 128 : (y0 + top) * 128 + 128] = t[96:144, : top * 128].astype(BF16)
+            low = max(y0, 1)
+            ty3[x, :, low * 128 : (y0 + CHUNK) * 128] = t[144:192, (low - y0) * 128 :].astype(BF16)
             for j in range(CHUNK):
                 at = slice((y0 + j) * 128, (y0 + j + 1) * 128)
                 tz4[x, :, at] = shift_lanes(t[192:240, j * 128 : (j + 1) * 128], False).astype(BF16)
                 tz5[x, :, at] = shift_lanes(t[240:288, j * 128 : (j + 1) * 128], True).astype(BF16)
 
-    def order(i):
-        return lax.rem(i * (cx - 1), cx)
-
-    def slab(i, _):
-        x, ahead = order(i), order(i + 1)
-
-        @pl.when(i < cx - 1)
-        def _():
-            adj_copy(ahead).wait()
-
-        vel_copy(x).wait()
-        traces(x)
-        sense(x)
-        turn(ahead)
+    def face(k):
+        return slice(192 + ROWS * k, 192 + ROWS * (k + 1))
+
+    def edge_x(k, turned, to):
+        for y0 in range(0, 16, CHUNK):
+            cols = jnp.concatenate([turned[y0 + j] for j in range(CHUNK)], axis=1)
+            got = jnp.dot(weights[face(k)], cols, preferred_element_type=F32)
+            to[:, y0 * 128 : (y0 + CHUNK) * 128] = got.astype(BF16)
+
+    def edge_y(k, y, to, at):
+        cols = jnp.concatenate([t[y] for t in turned], axis=1)
+        got = jnp.dot(weights[face(k)], cols, preferred_element_type=F32).astype(BF16)
+        for x in range(cx):
+            to[x, :, at : at + 128] = got[:, x * 128 : (x + 1) * 128]
+
+    def service():
         if remote:
-            @pl.when(i == 0)
-            def _():
-                pl.semaphore_wait(barrier, n_plane + n_line)
-                lax.fori_loop(1, n_plane, send_a, 0)
-                x_down.start()
-
-            @pl.when(i == 1)
-            def _():
-                x_up.start()
-
-        return 0
-
-    for c in small[:5]:
+            all_a.wait_recv()
+            total = slots_a[0]
+            for s in range(1, n_plane):
+                total = total + slots_a[s]
+            part_b[...] = total
+            slots_b[line] = total
+            send_to_all(in_line, part_b, slots_b.at[line], 1)
+
+    trace_copy.wait()
+    adj_copy(0).wait()
+    turn(0, turned[0])
+    edge_x(1, turned[0], tx1.at[0])
+    adj_copy(cx - 1).wait()
+    turn(cx - 1, turned[cx - 1])
+    edge_x(0, turned[cx - 1], tx0.at[cx])
+    for c in (den_copy, met_copy, ids_copy):
         c.wait()
-    weights[0:192, :] = vol[...].T
 
     weighted = den[...] * met[...]
     lane = lax.broadcasted_iota(jnp.int32, (1, 128), 1)
@@ -217,36 +204,59 @@
     if remote:
         slots_a[spot] = row
 
-    adj_copy(0).wait()
-    turn(0)
-    lax.fori_loop(0, cx, slab, 0)
+    if remote:
+        pl.semaphore_wait(barrier, n_plane + n_line)
+        send_to_all(in_plane, part_a, slots_a.at[spot], 0)
+        x_down.start()
+        x_up.start()
+    for x in (0, cx - 1, 2, 1):
+        vel_copy(x).start()
+    orient_copy.start()
+    lift_copy.start()
+    for x in (2, 1):
+        adj_copy(x).wait()
+        turn(x, turned[x])
+    edge_y(3, 0, ty3, 0)
+    edge_y(2, 15, ty2, 2048)
     if remote:
         @pl.when(span > 0)
         def _():
             y_down.start()
-            q_down.start()
 
         @pl.when(span < n_span - 1)
         def _():
             y_up.start()
-            q_up.start()
-
+
+    vol_copy.wait()
+    weights[0:192, :] = vol[...].T
+    traces(0, turned[0])
+    traces(cx - 1, turned[cx - 1])
+    vel_copy(0).wait()
+    vel_copy(cx - 1).wait()
+    traces(2, turned[2])
+    sense(0)
+    sense(cx - 1)
+    vel_copy(2).wait()
+    vel_copy(1).wait()
+    traces(1, turned[1])
+    sense(2)
+    sense(1)
+    lift_copy.wait()
+    lift_weights[...] = lift[...].T
+    orient_copy.wait()
+    sign[...] = 1.0 - 2.0 * orient[...].astype(F32)
+    service()
+    if remote:
         s_down.start()
         s_up.start()
 
-    small[6].wait()
-    lift_weights[...] = lift[...].T
-    small[5].wait()
-    sign[...] = 1.0 - 2.0 * orient[...].astype(F32)
-
-    if remote:
-        all_a.wait_recv()
-        total = slots_a[0]
-        for s in range(1, n_plane):
-            total = total + slots_a[s]
-        part_b[...] = total
-        slots_b[line] = total
-        lax.fori_loop(1, n_line, send_b, 0)
+        @pl.when(span > 0)
+        def _():
+            q_down.start()
+
+        @pl.when(span < n_span - 1)
+        def _():
+            q_up.start()
 
     @pl.when(span == 0)
     def _():
@@ -269,7 +279,7 @@
         def _():
             y_down.wait_recv()
 
-    def lifted(x):
+    def lifted(x, back):
         for y0 in range(0, 16, CHUNK):
             lanes = slice(y0 * 128, (y0 + CHUNK) * 128)
             later = slice(y0 * 128 + 128, (y0 + CHUNK) * 128 + 128)
@@ -280,30 +290,24 @@
                 parts.append(faces[k] * jnp.concatenate(rows, axis=1).astype(BF16))
             got = jnp.dot(lift_weights[...], jnp.concatenate(parts, axis=0), preferred_element_type=F32)
             for j in range(CHUNK):
-                back[x, y0 + j] = (base[x, y0 + j] + got[:, j * 128 : (j + 1) * 128]).astype(BF16)
-
-    def turn_back(x):
+                back[y0 + j] = (base[x, y0 + j] + got[:, j * 128 : (j + 1) * 128]).astype(BF16)
+
+    def turn_back(x, back):
         for d in range(0, 192, 16):
-            held[d : d + 16, x] = jnp.swapaxes(back[x, :, d : d + 16], 0, 1)
-
-    def late(i):
-        return jnp.where(i < 2, i + 1, (cx - 1) * (i - 2))
-
-    def finish(i, _):
-        if remote:
-            @pl.when(i == 2)
-            def _():
-                x_down.wait_recv()
-                x_up.wait_recv()
-
-        x = late(i)
-        before = late(jnp.maximum(i - 1, 0))
-        lifted(x)
-        turn_back(before)
-        return 0
-
-    lax.fori_loop(0, cx, finish, 0)
-    turn_back(late(cx - 1))
+            held[d : d + 16, x] = jnp.swapaxes(back[:, d : d + 16], 0, 1)
+
+    lifted(1, back_a)
+    lifted(2, back_b)
+    turn_back(1, back_a)
+    if remote:
+        x_up.wait_recv()
+    lifted(0, back_a)
+    turn_back(2, back_b)
+    if remote:
+        x_down.wait_recv()
+    lifted(cx - 1, back_b)
+    turn_back(0, back_a)
+    turn_back(cx - 1, back_b)
 
     if remote:
         @pl.when(span > 0)
@@ -398,8 +402,7 @@
             pltpu.VMEM((480, 192), BF16),
             pltpu.VMEM((192, 288), BF16),
             pltpu.VMEM((6, *cells), F32),
-            pltpu.VMEM((cx, 16, 192, 128), BF16),
-            pltpu.VMEM((cx, 16, 192, 128), BF16),
+            *[pltpu.VMEM((16, 192, 128), BF16)] * 6,
             pltpu.VMEM((cx, 16, 192, 128), F32),
             pltpu.VMEM((cx + 1, ROWS, 2048), BF16),
             pltpu.VMEM((cx + 1, ROWS, 2048), BF16),

time: 25.6 us -> 23.9 us (0.934)
  Pallas kernels: 24.9 us -> 23.1 us
    pallas_call x1, Pallas kernels: 22.6 us -> 20.8 us  [shards(): pl.pallas_call(functools.partial(first_kernel, n_stream, n_span, remote),...]
where the time goes in v3:
time: 23.9 us; the launch traced here: 23.8 us
  Pallas kernels  23.1 us (97%)
  between operations  0.64 us (3%)
    pallas_call x1, Pallas kernels, shards(): pl.pallas_call(functools.partial(first_kernel, n_stream, n_span, remote),...  20.8 us
    pallas_call x1, Pallas kernels, shards(): pl.pallas_call(second_kernel, out_shape=[jax.ShapeDtypeStruct(adjoint.sha...  2.35 us

profile of v3, /device:TPU:1, one launch (start us, length us, event | category | flops | bytes accessed | tf_op | source)
XLA Modules:
  0.0 23.8 jit_solution(15469675224242915046)
XLA Ops:
  0.6 20.8 %shard_map.112 = (bf16[192,4,16,128]{3,2,1,0:T(8,128)(2,1)S(1)}, f32[4,16,128]{2,1,0:T(8,128)S(1)}, f32[1,128]{1,0:T(1,128)S(1)}) custom-call(bf16[192,4,16,128]{3,2,1,0:T(8,128)(2,1)} %adj_hbm.1, bf16[192,4,16,128]{3,2,1,0:T(8,128)(2,1)} %vel_hbm.1, f32[4,16,128]{2,1,0:T(8,128)} %den_hbm.1, f32[4,16,128]{2,1,0:T(8,128)} %met_hbm.1, s32[4,16,128]{2,1,0:T(8,128)} %ids_hbm.1, ...), custom_call_target="tpu_custom_call" | custom-call | tf_op jit(solution)/shard_map/pallas_call | solution.py:388
  21.4 2.3 %shard_map.113 = (bf16[192,4,16,128]{3,2,1,0:T(8,128)(2,1)}, f32[4,16,128]{2,1,0:T(8,128)}, f32[4]{0:T(128)}) custom-call(bf16[192,4,16,128]{3,2,1,0:T(8,128)(2,1)S(1)} %get-tuple-element.6.held, f32[4,16,128]{2,1,0:T(8,128)S(1)} %get-tuple-element.7.filt_in, f32[1,128]{1,0:T(1,128)S(1)} %get-tuple-element.8.vol_in), custom_call_target="tpu_custom_call" | custom-call | tf_op jit(solution)/shard_map/pallas_call | solution.py:430

commit v4 on v3

--- a/solution.py
+++ b/solution.py
@@ -245,7 +245,6 @@
     lift_weights[...] = lift[...].T
     orient_copy.wait()
     sign[...] = 1.0 - 2.0 * orient[...].astype(F32)
-    service()
     if remote:
         s_down.start()
         s_up.start()
@@ -257,6 +256,8 @@
         @pl.when(span < n_span - 1)
         def _():
             q_up.start()
+
+    service()
 
     @pl.when(span == 0)
     def _():
@@ -299,33 +300,44 @@
     lifted(1, back_a)
     lifted(2, back_b)
     turn_back(1, back_a)
-    if remote:
-        x_up.wait_recv()
-    lifted(0, back_a)
+    core = lax.rem(stream, 2)
+    soon = (1 - core) * (cx - 1)
+    late = core * (cx - 1)
+    if remote:
+        @pl.when(core == 0)
+        def _():
+            x_down.wait_recv()
+
+        @pl.when(core == 1)
+        def _():
+            x_up.wait_recv()
+
+    lifted(soon, back_a)
     turn_back(2, back_b)
-    if remote:
-        x_down.wait_recv()
-    lifted(cx - 1, back_b)
-    turn_back(0, back_a)
-    turn_back(cx - 1, back_b)
+    turn_back(soon, back_a)
+    if remote:
+        @pl.when(core == 0)
+        def _():
+            x_up.wait_recv()
+
+        @pl.when(core == 1)
+        def _():
+            x_down.wait_recv()
+
+    lifted(late, back_b)
+    turn_back(late, back_b)
 
     if remote:
         @pl.when(span > 0)
         def _():
-            y_down.wait_send()
-            q_down.wait_send()
             q_up.wait_recv()
 
         @pl.when(span < n_span - 1)
         def _():
-            y_up.wait_send()
-            q_up.wait_send()
             q_down.wait_recv()
 
-        s_down.wait()
-        s_up.wait()
-        x_down.wait_send()
-        x_up.wait_send()
+        s_down.wait_recv()
+        s_up.wait_recv()
     else:
         for r in (sx_lo, sx_hi, sy_lo, sy_hi):
             r[...] = jnp.zeros_like(r)
@@ -338,6 +350,22 @@
         beside = beside + shift_rows(own, sy_lo[x : x + 1], False) + shift_rows(own, sy_hi[x : x + 1], True)
         beside = beside + shift_lanes(own, False) + shift_lanes(own, True)
         filt[x] = (own + FILTER_BETA * beside) / (1.0 + 6.0 * FILTER_BETA)
+
+    if remote:
+        @pl.when(span > 0)
+        def _():
+            y_down.wait_send()
+            q_down.wait_send()
+
+        @pl.when(span < n_span - 1)
+        def _():
+            y_up.wait_send()
+            q_up.wait_send()
+
+        s_down.wait_send()
+        s_up.wait_send()
+        x_down.wait_send()
+        x_up.wait_send()
 
     if remote:
         all_b.wait_recv()

time: 23.9 us -> 23.5 us (0.983)
  Pallas kernels: 23.1 us -> 22.6 us
    pallas_call x1, Pallas kernels: 20.8 us -> 20.2 us  [shards(): pl.pallas_call(functools.partial(first_kernel, n_stream, n_span, remote),...]
where the time goes in v4:
time: 23.5 us; the launch traced here: 23.2 us
  Pallas kernels  22.6 us (96%)
  between operations  0.64 us (3%)
    pallas_call x1, Pallas kernels, shards(): pl.pallas_call(functools.partial(first_kernel, n_stream, n_span, remote),...  20.2 us
    pallas_call x1, Pallas kernels, shards(): pl.pallas_call(second_kernel, out_shape=[jax.ShapeDtypeStruct(adjoint.sha...  2.35 us

profile of v4, /device:TPU:1, one launch (start us, length us, event | category | flops | bytes accessed | tf_op | source)
XLA Modules:
  0.0 23.2 jit_solution(11173363120902301244)
XLA Ops:
  0.6 20.2 %shard_map.112 = (bf16[192,4,16,128]{3,2,1,0:T(8,128)(2,1)S(1)}, f32[4,16,128]{2,1,0:T(8,128)S(1)}, f32[1,128]{1,0:T(1,128)S(1)}) custom-call(bf16[192,4,16,128]{3,2,1,0:T(8,128)(2,1)} %adj_hbm.1, bf16[192,4,16,128]{3,2,1,0:T(8,128)(2,1)} %vel_hbm.1, f32[4,16,128]{2,1,0:T(8,128)} %den_hbm.1, f32[4,16,128]{2,1,0:T(8,128)} %met_hbm.1, s32[4,16,128]{2,1,0:T(8,128)} %ids_hbm.1, ...), custom_call_target="tpu_custom_call" | custom-call | tf_op jit(solution)/shard_map/pallas_call | solution.py:416
  20.9 2.3 %shard_map.113 = (bf16[192,4,16,128]{3,2,1,0:T(8,128)(2,1)}, f32[4,16,128]{2,1,0:T(8,128)}, f32[4]{0:T(128)}) custom-call(bf16[192,4,16,128]{3,2,1,0:T(8,128)(2,1)S(1)} %get-tuple-element.6.held, f32[4,16,128]{2,1,0:T(8,128)S(1)} %get-tuple-element.7.filt_in, f32[1,128]{1,0:T(1,128)S(1)} %get-tuple-element.8.vol_in), custom_call_target="tpu_custom_call" | custom-call | tf_op jit(solution)/shard_map/pallas_call | solution.py:458

commit v5 on v4

--- a/solution.py
+++ b/solution.py
@@ -280,18 +280,27 @@
         def _():
             y_down.wait_recv()
 
-    def lifted(x, back):
+    def lifted(x, back, chosen=tuple(range(6)), last=True):
+        if len(chosen) == 6:
+            block = lift_weights[...]
+        else:
+            block = jnp.concatenate([lift[ROWS * k : ROWS * (k + 1)] for k in chosen], axis=0).T
         for y0 in range(0, 16, CHUNK):
             lanes = slice(y0 * 128, (y0 + CHUNK) * 128)
             later = slice(y0 * 128 + 128, (y0 + CHUNK) * 128 + 128)
-            faces = (tx0[x, :, lanes], tx1[x + 1, :, lanes], ty2[x, :, lanes], ty3[x, :, later], tz4[x, :, lanes], tz5[x, :, lanes])
+            faces = ((tx0, x, lanes), (tx1, x + 1, lanes), (ty2, x, lanes), (ty3, x, later), (tz4, x, lanes), (tz5, x, lanes))
             parts = []
-            for k in range(6):
+            for k in chosen:
+                ref, at, cut = faces[k]
                 rows = [jnp.broadcast_to(sign[k, x, y0 + j : y0 + j + 1], (ROWS, 128)) for j in range(CHUNK)]
-                parts.append(faces[k] * jnp.concatenate(rows, axis=1).astype(BF16))
-            got = jnp.dot(lift_weights[...], jnp.concatenate(parts, axis=0), preferred_element_type=F32)
+                parts.append(ref[at, :, cut] * jnp.concatenate(rows, axis=1).astype(BF16))
+            got = jnp.dot(block, jnp.concatenate(parts, axis=0), preferred_element_type=F32)
             for j in range(CHUNK):
-                back[y0 + j] = (base[x, y0 + j] + got[:, j * 128 : (j + 1) * 128]).astype(BF16)
+                total = base[x, y0 + j] + got[:, j * 128 : (j + 1) * 128]
+                if last:
+                    back[y0 + j] = total.astype(BF16)
+                else:
+                    base[x, y0 + j] = total
 
     def turn_back(x, back):
         for d in range(0, 192, 16):
@@ -315,16 +324,21 @@
     lifted(soon, back_a)
     turn_back(2, back_b)
     turn_back(soon, back_a)
-    if remote:
-        @pl.when(core == 0)
-        def _():
+
+    @pl.when(core == 0)
+    def _():
+        lifted(0, back_b, (1, 2, 3, 4, 5), False)
+        if remote:
             x_up.wait_recv()
-
-        @pl.when(core == 1)
-        def _():
+        lifted(0, back_b, (0,))
+
+    @pl.when(core == 1)
+    def _():
+        lifted(cx - 1, back_b, (0, 2, 3, 4, 5), False)
+        if remote:
             x_down.wait_recv()
-
-    lifted(late, back_b)
+        lifted(cx - 1, back_b, (1,))
+
     turn_back(late, back_b)
 
     if remote:

time: 23.5 us -> 23.7 us (level)
  no operation moved by 1% of the time
where the time goes in v5:
time: 23.7 us; the launch traced here: 23.4 us
  Pallas kernels  22.8 us (96%)
  between operations  0.64 us (3%)
    pallas_call x1, Pallas kernels, shards(): pl.pallas_call(functools.partial(first_kernel, n_stream, n_span, remote),...  20.4 us
    pallas_call x1, Pallas kernels, shards(): pl.pallas_call(second_kernel, out_shape=[jax.ShapeDtypeStruct(adjoint.sha...  2.35 us

profile of v5, /device:TPU:1, one launch (start us, length us, event | category | flops | bytes accessed | tf_op | source)
XLA Modules:
  0.0 23.4 jit_solution(7491997839892963675)
XLA Ops:
  0.6 20.4 %shard_map.112 = (bf16[192,4,16,128]{3,2,1,0:T(8,128)(2,1)S(1)}, f32[4,16,128]{2,1,0:T(8,128)S(1)}, f32[1,128]{1,0:T(1,128)S(1)}) custom-call(bf16[192,4,16,128]{3,2,1,0:T(8,128)(2,1)} %adj_hbm.1, bf16[192,4,16,128]{3,2,1,0:T(8,128)(2,1)} %vel_hbm.1, f32[4,16,128]{2,1,0:T(8,128)} %den_hbm.1, f32[4,16,128]{2,1,0:T(8,128)} %met_hbm.1, s32[4,16,128]{2,1,0:T(8,128)} %ids_hbm.1, ...), custom_call_target="tpu_custom_call" | custom-call | tf_op jit(solution)/shard_map/pallas_call | solution.py:430
  21.1 2.3 %shard_map.113 = (bf16[192,4,16,128]{3,2,1,0:T(8,128)(2,1)}, f32[4,16,128]{2,1,0:T(8,128)}, f32[4]{0:T(128)}) custom-call(bf16[192,4,16,128]{3,2,1,0:T(8,128)(2,1)S(1)} %get-tuple-element.6.held, f32[4,16,128]{2,1,0:T(8,128)S(1)} %get-tuple-element.7.filt_in, f32[1,128]{1,0:T(1,128)S(1)} %get-tuple-element.8.vol_in), custom_call_target="tpu_custom_call" | custom-call | tf_op jit(solution)/shard_map/pallas_call | solution.py:472
